TPU v7x, 256 devices: a whole 4x4x8 slice. The times are simulated.
256 devices in a mesh: pair: 64 (over x, y, z_lo), orb: 4 (over z_hi, core).
Axes of the slice: x: 4, y: 4, z: 8 (z_hi: 2, z_lo: 4; z = z_hi * 4 + z_lo), core: 2. Of those that a mesh axis runs over, the one named last changes fastest.
Arguments:
- ao_slab: bfloat16 [512, 1224, 1224], P('pair', 'orb'), may hold values from -9 to 9, as said below
- occ_coef: bfloat16 [1224, 200], replicated, may hold values from -0.15625 to 0.15625
- vir_coef: bfloat16 [1224, 1024], P(None, 'orb'), may hold values from -1.5 to 1.5
- tile_index: int32 [16], replicated, may hold values from 0 to 1223
- pair_order: int32 [20160], replicated, may hold values from 0 to 20159, each once
Outputs:
- mixed_block: bfloat16 [20160, 32, 1024], P('pair', None, 'orb')
Inputs may be any that keep to these rules, and one draw needn't show every extreme that they name: ao_slab[rs, p, q] equals ao_slab[rs, q, p].
All inputs are finite; a program needn't handle non-finite values.
Results may differ from a plain program's by a relative error of at most 0.0057.
Values may be sent and summed in bfloat16 or wider, within the bound.
No kernel may reach another device: no remote copies, remote signals or barrier semaphores. Data moves between devices by JAX's collectives and lax.ppermute only.
A program may use at most 128 MiB of HBM per device.

v0:
```python
import jax
import jax.numpy as jnp
import numpy as np
from jax import lax
from jax.sharding import PartitionSpec as P


def on_device(ao_slab, occ_coef, vir_coef, tile_index, pair_order):
    orb_pos = lax.axis_index("orb")
    slab_rows = ao_slab.shape[1]
    local_pairs = ao_slab.shape[0]
    n_pair = lax.axis_size("pair")
    nocc = occ_coef.shape[1]
    packed_count = nocc * (nocc + 1) // 2
    padded = pair_order.shape[0]
    owned = padded // n_pair
    lower = np.tril_indices(nocc)
    packed_cols = jnp.asarray((lower[0] * nocc + lower[1]).astype(np.int32))
    valid = (pair_order < packed_count).astype(jnp.float32)
    columns_all = packed_cols[jnp.minimum(pair_order, packed_count - 1)]
    occ_rows = lax.dynamic_slice_in_dim(occ_coef, orb_pos * slab_rows, slab_rows, 0)
    first_half = jnp.einsum(
        "kpq,qj->kpj", ao_slab, occ_coef, preferred_element_type=jnp.float32
    ).astype(jnp.bfloat16)
    partial_value = jnp.einsum(
        "pi,kpj->kij", occ_rows, first_half, preferred_element_type=jnp.float32
    )
    partial_value = partial_value.reshape(local_pairs, nocc * nocc)
    ordered = (partial_value[:, columns_all] * valid).reshape(local_pairs, n_pair, owned)
    total = lax.psum(ordered, "orb").astype(jnp.bfloat16)
    received = lax.all_to_all(total, "pair", split_axis=1, concat_axis=0, tiled=True)
    gathered = received.reshape(local_pairs * n_pair, owned)
    tile_width = tile_index.shape[0]
    grid = gathered.reshape(gathered.shape[0] // tile_width, tile_width, owned)
    vir_rows = vir_coef[tile_index]
    result = jnp.einsum("rsp,sb->prb", grid, vir_rows, preferred_element_type=jnp.float32)
    return result.astype(jnp.bfloat16)


def solution(mesh):
    return jax.shard_map(
        on_device,
        mesh=mesh,
        in_specs=(P("pair", "orb", None), P(), P(None, "orb"), P(), P()),
        out_specs=P("pair", None, "orb"),
        check_vma=False,
    )
```

profile of v0, /device:TPU:1, one launch (start us, length us, event | category | flops | bytes accessed | tf_op | source)
XLA Modules:
  0.0 247.3 jit_solution(1863390080722365165)
XLA Ops:
  0.0 0.0 copy-start
  0.0 1.0 compare_select_fusion.1
  1.0 0.9 compare_convert_fusion
  1.9 6.0 %convolution_bitcast_fusion = f32[8,200,200]{1,2,0:T(8,128)S(1)} fusion(bf16[8,306,1224]{2,0,1:T(8,128)(2,1)} %param.6, bf16[1224,200]{0,1:T(8,128)(2,1)} %param.7, s32[]{:T(128)S(6)} %select_n.20), kind=kOutput, calls=%fused_computation.7 | convolution fusion | flops 1394870400 | bytes 8212484 | tf_op jit(solution)/shard_map/pi,kpj->kij/dot_general | solution.py:25
  7.9 0.0 copy-start.1
  7.9 10.9 %copy.20 = f32[8,200,200]{0,2,1:T(8,128)} copy(f32[8,200,200]{1,2,0:T(8,128)S(1)} %convolution_bitcast_fusion) | data formatting | bytes 2560000 | tf_op jit(solution)/shard_map/reshape | solution.py:28
  18.8 0.0 copy-done.1
  18.8 103.6 %gather_fusion.1 = s32[20160]{0:T(1024)S(1)} fusion(s32[20100]{0:T(1024)S(1)} %copy-done.1, s32[20480]{0:T(1024)S(1)} %pad_clamp_fusion.1), kind=kCustom, calls=%fused_computation.1 | custom fusion | bytes 241920 | tf_op jit(solution)/shard_map/gather | solution.py:20
  122.4 0.2 fusion.11
  122.6 44.6 %gather_fusion.2 = f32[20160,8]{1,0:T(8,128)} fusion(f32[8,40000]{0,1:T(8,128)} %bitcast.22, s32[20480]{0:T(1024)S(1)} %pad_clamp_fusion), kind=kCustom, calls=%fused_computation.2 | custom fusion | bytes 1370880 | tf_op jit(solution)/shard_map/gather | solution.py:29
  167.3 0.0 copy-start.2
  167.3 6.4 %copy.17 = f32[8,20160]{1,0:T(8,128)S(1)} copy(f32[8,20160]{0,1:T(8,128)} %bitcast.23) | data formatting | bytes 1290240 | tf_op jit(solution)/shard_map/gather | solution.py:29
  173.6 0.7 gather.17
  174.4 0.2 reshape.27
  174.6 0.1 broadcast_multiply_fusion
  174.6 40.9 %all-reduce.1 = bf16[8,64,315]{2,1,0:T(8,128)(2,1)S(1)} all-reduce(f32[8,64,315]{2,1,0:T(8,128)S(1)} %broadcast_multiply_fusion), channel_id=1, replica_groups=mesh['pair'=64,'orb'=4] {'orb'}, use_global_device_ids=true, to_apply=%region_0.0 | all-reduce | flops 161280 | bytes 967680 | tf_op jit(solution)/shard_map/psum | solution.py:30
  215.6 1.0 copy.18
  216.5 9.4 %all-to-all-start = ((bf16[8,64,315]{2,0,1:T(8,128)(2,1)}), bf16[8,64,315]{2,0,1:T(8,128)(2,1)S(1)}, u32[]{:S(2)}, u32[]{:S(2)}) async-start(bf16[8,64,315]{2,0,1:T(8,128)(2,1)} %copy.18), calls=%async_computation | async-start | bytes 786432 | tf_op jit(solution)/shard_map/all_to_all | solution.py:31
  226.0 0.0 copy-done.2
  226.0 0.0 copy-done
  226.0 0.6 gather_fusion
  226.6 13.8 %all-to-all-done = bf16[8,64,315]{2,0,1:T(8,128)(2,1)S(1)} async-done(((bf16[8,64,315]{2,0,1:T(8,128)(2,1)}), bf16[8,64,315]{2,0,1:T(8,128)(2,1)S(1)}, u32[]{:S(2)}, u32[]{:S(2)}) %all-to-all-start) | async-done | bytes 322592 | tf_op jit(solution)/shard_map/all_to_all | solution.py:31
  240.4 1.6 convert_bitcast_fusion
  242.0 5.3 %copy.19 = bf16[315,32,256]{2,1,0:T(8,128)(2,1)} copy(bf16[315,32,256]{2,0,1:T(8,128)(2,1)S(1)} %convert_bitcast_fusion) | data formatting | bytes 10321920 | tf_op jit(solution)/shard_map/convert_element_type | solution.py:37
  (4 shorter events, 0.0 us)
Async XLA Ops:
  0.0 226.0 %copy-start = (bf16[1224,256]{1,0:T(8,128)(2,1)S(1)}, bf16[1224,256]{1,0:T(8,128)(2,1)}, u32[]{:S(2)}) copy-start(bf16[1224,256]{1,0:T(8,128)(2,1)} %param.8) | copy-start | bytes 1880068
  7.9 10.9 %copy-start.1 = (s32[20100]{0:T(1024)S(1)}, s32[20100]{0:T(1024)}, u32[]{:S(2)}) copy-start(s32[20100]{0:T(1024)} %constant.5.clone) | copy-start | bytes 241204
  167.3 58.7 %copy-start.2 = (s32[16]{0:T(128)S(1)}, s32[16]{0:T(128)}, u32[]{:S(2)}) copy-start(s32[16]{0:T(128)} %param.9) | copy-start | bytes 196
  216.5 23.9 %all-to-all-start = ((bf16[8,64,315]{2,0,1:T(8,128)(2,1)}), bf16[8,64,315]{2,0,1:T(8,128)(2,1)S(1)}, u32[]{:S(2)}, u32[]{:S(2)}) async-start(bf16[8,64,315]{2,0,1:T(8,128)(2,1)} %copy.18), calls=%async_computation | async-start | bytes 786432 | tf_op jit(solution)/shard_map/all_to_all | solution.py:31
where the time goes:
time: 248 us; the launch traced here: 247 us
  local copies, waits for them, and re-layouts  173 us (70%)
  blocking collectives  40.9 us (16%)
  waiting for transfers between devices  13.8 us (6%)
  starting transfers between devices  9.44 us (4%)
  matrix products  7.59 us (3%)
    gather x1, local copies, waits for them, and re-layouts, on_device(): columns_all = packed_cols[jnp.minimum(pair_order, packed_count - 1)]  104 us
    gather x3, local copies, waits for them, and re-layouts, on_device(): partial_value[:, columns_all] * valid  51.7 us
    psum x1, blocking collectives, on_device(): total = lax.psum(ordered, 'orb').astype(jnp.bfloat16)  40.9 us
    all_to_all x1, waiting for transfers between devices, on_device(): lax.all_to_all(total, 'pair', split_axis=1, concat_axis=0, tiled=True)  13.8 us
    reshape x1, local copies, waits for them, and re-layouts, on_device(): partial_value = partial_value.reshape(local_pairs, nocc * nocc)  10.9 us
    all_to_all x1, starting transfers between devices, on_device(): lax.all_to_all(total, 'pair', split_axis=1, concat_axis=0, tiled=True)  9.44 us
    dot_general x1, matrix products, on_device(): jnp.einsum('pi,kpj->kij', occ_rows, first_half, preferred_element_type=jn...  6.01 us
    convert_element_type x1, local copies, waits for them, and re-layouts, on_device(): return result.astype(jnp.bfloat16)  5.33 us
  transfers between devices with their start and end apart: 1, of which 1 were waited for; matrix products, arithmetic and copies ran while one was open for 0% of the time, Pallas kernels for 0%

commit v1 on v0

v1 whole, which is shorter than its diff:
```python
import jax
import jax.numpy as jnp
from jax import lax
from jax.experimental import pallas as pl
from jax.experimental.pallas import tpu as pltpu
from jax.sharding import PartitionSpec as P

NOCC = 200
COLS = 88
ROWS = 256
NPAIRS = NOCC * (NOCC + 1) // 2
KPER = 4
SLOT = 320
CHUNK = 4 * SLOT


def fold(pair_order):
    t = pair_order
    root = jnp.sqrt(8.0 * t.astype(jnp.float32) + 1.0)
    i = ((root - 1.0) * 0.5).astype(jnp.int32)
    i = jnp.where(i * (i + 1) // 2 > t, i - 1, i)
    i = jnp.where((i + 1) * (i + 2) // 2 <= t, i + 1, i)
    j = t - i * (i + 1) // 2
    row = jnp.where(j < 88, i, jnp.where(j >= 113, j - 113, jnp.where(i >= 112, j + 112, j + 137)))
    col = jnp.where(j < 88, j, jnp.where((j >= 113) | (i >= 112), i - 112, i - 88))
    return row, jnp.where(t < NPAIRS, col, -1)


def half_kernel(core_ref, ao_ref, ct_ref, ctp_ref, keep_ref, send_ref, first_ref):
    step = pl.program_id(0)
    block, kk, nq = ao_ref.shape
    slab = ao_ref[...].reshape(block * kk, nq)
    first = lax.dot_general(slab, ct_ref[...], (((1,), (1,)), ((), ())), preferred_element_type=jnp.float32)
    at = pl.ds(pl.multiple_of(step * (block * kk), 8), block * kk)
    first_ref[0, at, :] = first[:, 0:128]
    first_ref[1, at, 0:NOCC - 128] = first[:, 128:NOCC]

    @pl.when(step == pl.num_programs(0) - 1)
    def _():
        core = core_ref[0]
        np_ = first_ref.shape[1] // kk
        lane = lax.broadcasted_iota(jnp.int32, (COLS, ROWS), 1)
        col = lax.broadcasted_iota(jnp.int32, (COLS, ROWS), 0)
        ctp = ctp_ref[...]

        def folded(k):
            at = pl.ds(k, np_, stride=kk)
            fk = jnp.concatenate([first_ref[0, at, :], first_ref[1, at, :]], axis=1)
            fk = jnp.where(lax.broadcasted_iota(jnp.int32, fk.shape, 1) < NOCC, fk, 0.0).astype(jnp.bfloat16)
            out = jnp.dot(ctp, fk, preferred_element_type=jnp.float32)
            o1 = out[0:88]
            o2 = out[88:176]
            o3 = jnp.concatenate([out[176:200], jnp.zeros((64, ROWS), jnp.float32)], axis=0)
            tri = jnp.where(lane >= col, o1, pltpu.roll(o2, ROWS - 113, 1))
            rest = jnp.where(lane < 225, pltpu.roll(o2, 112, 1), pltpu.roll(o3, 137, 1))
            return jnp.where(lane < NOCC, tri, jnp.where(lane < 249, rest, 0.0))

        for k in range(KPER):
            send_ref[k] = folded(KPER * (1 - core) + k).astype(jnp.bfloat16)
        for k in range(KPER):
            keep_ref[k] = folded(KPER * core + k)


def select_kernel(row_ref, col_ref, keep_ref, recv_ref, out_ref, tri_ref):
    for k in range(KPER):
        tri_ref[k * COLS:(k + 1) * COLS, :] = (keep_ref[k] + recv_ref[k].astype(jnp.float32)).astype(jnp.bfloat16)

    @pl.loop(0, row_ref.shape[0])
    def _(ch):
        row = row_ref[ch]
        col = col_ref[ch]
        hot = (lax.broadcasted_iota(jnp.int32, (ROWS, CHUNK), 0) == row).astype(jnp.bfloat16)
        picked = jnp.dot(tri_ref[...], hot, preferred_element_type=jnp.float32)
        mask = lax.broadcasted_iota(jnp.int32, (COLS, CHUNK), 0) == col
        vals = [
            jnp.sum(jnp.where(mask, picked[k * COLS:(k + 1) * COLS], 0.0), axis=0, keepdims=True)
            for k in range(KPER)
        ]
        vals = jnp.concatenate(vals, axis=0)
        lane = lax.broadcasted_iota(jnp.int32, (2, 2 * SLOT), 1)
        for u in range(2):
            here = vals[:, 2 * SLOT * u:2 * SLOT * (u + 1)]
            moved = pltpu.roll(here, SLOT, 1)
            even = jnp.where(lane < SLOT, here[0:2], moved[2:4]).astype(jnp.bfloat16)
            odd = jnp.where(lane < SLOT, moved[0:2], here[2:4]).astype(jnp.bfloat16)
            at = ch * 8 + u * 4
            out_ref[at] = even
            out_ref[at + 1] = even
            out_ref[at + 2] = odd
            out_ref[at + 3] = odd


def final_kernel(core_ref, own_ref, other_ref, vir_ref, out_ref, turned_ref, vbig_ref):
    step = pl.program_id(0)
    block = out_ref.shape[0]

    @pl.when(step == 0)
    def _():
        core = core_ref[0]
        line = lax.broadcasted_iota(jnp.int32, (256, 16), 0)
        s = lax.broadcasted_iota(jnp.int32, (256, 16), 1)
        src_core = jnp.where(line < 128, core, 1 - core)
        want = ((line % 8) // 4) * 8 + 4 * src_core + line % 2 + 2 * ((line % 128) // 64)
        hot = (s == want).astype(jnp.bfloat16)
        vbig_ref[...] = jnp.dot(hot, vir_ref[...], preferred_element_type=jnp.float32).astype(jnp.bfloat16)
        for g in range(4):
            for n, ref in enumerate((own_ref, other_ref)):
                part = ref[32 * g:32 * (g + 1)].astype(jnp.float32).reshape(64, 2 * SLOT)
                wide = jnp.concatenate([part[:, 0:SLOT], part[:, SLOT:2 * SLOT]], axis=0)
                turned_ref[g, :, 128 * n:128 * (n + 1)] = wide.T

    lane = lax.broadcasted_iota(jnp.int32, (8, 256), 1)
    mask = (lane % 64) // 8 == lax.broadcasted_iota(jnp.int32, (8, 256), 0)
    at = pl.multiple_of(step * block, 8)
    for pair in range(2):
        parts = []
        for g in (2 * pair, 2 * pair + 1):
            rows = turned_ref[g, pl.ds(at, block), :]
            parts.append(jnp.where(mask[None], jnp.broadcast_to(rows[:, None, :], (block, 8, 256)), 0.0))
        lhs = jnp.concatenate(parts, axis=1).reshape(block * 16, 256).astype(jnp.bfloat16)
        res = jnp.dot(lhs, vbig_ref[...], preferred_element_type=jnp.float32)
        out_ref[:, 16 * pair:16 * (pair + 1), :] = res.reshape(block, 16, 256).astype(jnp.bfloat16)


def half_stage(core, slab, ct, ctp):
    np_, kk, nq = slab.shape
    block = 51
    kept = pl.BlockSpec((KPER, COLS, ROWS), lambda i: (0, 0, 0))
    return pl.pallas_call(
        half_kernel,
        grid=(np_ // block,),
        in_specs=[
            pl.BlockSpec(memory_space=pltpu.SMEM),
            pl.BlockSpec((block, kk, nq), lambda i: (i, 0, 0)),
            pl.BlockSpec((NOCC, nq), lambda i: (0, 0)),
            pl.BlockSpec((NOCC, np_), lambda i: (0, 0)),
        ],
        out_specs=[kept, kept],
        out_shape=[
            jax.ShapeDtypeStruct((KPER, COLS, ROWS), jnp.float32),
            jax.ShapeDtypeStruct((KPER, COLS, ROWS), jnp.bfloat16),
        ],
        scratch_shapes=[pltpu.VMEM((2, np_ * kk, 128), jnp.float32)],
        compiler_params=pltpu.CompilerParams(vmem_limit_bytes=48 * 2**20),
        name="half",
    )(core, slab, ct, ctp)


def places_of(pair_order, n_pair):
    owned = pair_order.shape[0] // n_pair
    row, col = fold(pair_order)
    pads = ((0, 0), (0, SLOT - owned))
    row = jnp.pad(row.reshape(n_pair, owned), pads).reshape(-1, 1, CHUNK)
    col = jnp.pad(col.reshape(n_pair, owned), pads, constant_values=-1).reshape(-1, 1, CHUNK)
    return row, col


def select_stage(row, col, keep, recv):
    n_dest = 2 * row.shape[0] * CHUNK // SLOT
    return pl.pallas_call(
        select_kernel,
        out_shape=jax.ShapeDtypeStruct((n_dest, 2, 2 * SLOT), jnp.bfloat16),
        in_specs=[pl.BlockSpec(memory_space=pltpu.VMEM)] * 4,
        out_specs=pl.BlockSpec(memory_space=pltpu.VMEM),
        scratch_shapes=[pltpu.VMEM((KPER * COLS, ROWS), jnp.bfloat16)],
        compiler_params=pltpu.CompilerParams(vmem_limit_bytes=48 * 2**20),
        name="select",
    )(row, col, keep, recv)


def final_stage(core, own, other, vir_rows, owned):
    block = 40
    full = pl.BlockSpec(own.shape, lambda i: (0, 0, 0))
    return pl.pallas_call(
        final_kernel,
        grid=(pl.cdiv(owned, block),),
        in_specs=[
            pl.BlockSpec(memory_space=pltpu.SMEM),
            full,
            full,
            pl.BlockSpec((16, 256), lambda i: (0, 0)),
        ],
        out_specs=pl.BlockSpec((block, 32, 256), lambda i: (i, 0, 0)),
        out_shape=jax.ShapeDtypeStruct((owned, 32, 256), jnp.bfloat16),
        scratch_shapes=[pltpu.VMEM((4, SLOT, 256), jnp.float32), pltpu.VMEM((256, 256), jnp.bfloat16)],
        compiler_params=pltpu.CompilerParams(vmem_limit_bytes=48 * 2**20),
        name="final",
    )(core, own, other, vir_rows)


def coef_rows(ct, start, size):
    part = lax.dynamic_slice_in_dim(ct, start, size, 1)
    return jnp.concatenate([part[0:88], part[112:200], part[88:112]], axis=0)


def on_device(ao_slab, occ_coef, vir_coef, tile_index, pair_order):
    orb = lax.axis_index("orb")
    core = (orb % 2).astype(jnp.int32).reshape(1)
    n_pair = lax.axis_size("pair")
    n_orb = lax.axis_size("orb")
    owned = pair_order.shape[0] // n_pair
    other_core = [(o, o ^ 1) for o in range(n_orb)]

    slab = jnp.transpose(ao_slab, (1, 0, 2))
    ct = occ_coef.T
    ctp = coef_rows(ct, orb * slab.shape[0], slab.shape[0])
    keep, send = half_stage(core, slab, ct, ctp)
    recv = lax.ppermute(send, "orb", other_core)
    row, col = places_of(pair_order, n_pair)
    blocks = select_stage(row, col, keep, recv)
    groups = [[p * n_orb + z * 2 + c for p in range(n_pair) for z in range(n_orb // 2)] for c in range(2)]
    own = lax.all_to_all(blocks, ("pair", "orb"), 0, 0, axis_index_groups=groups, tiled=True)
    other = lax.ppermute(own, "orb", other_core)
    vir_rows = vir_coef[tile_index]
    return final_stage(core, own, other, vir_rows, owned)


def solution(mesh):
    return jax.shard_map(
        on_device,
        mesh=mesh,
        in_specs=(P("pair", "orb", None), P(), P(None, "orb"), P(), P()),
        out_specs=P("pair", None, "orb"),
        check_vma=False,
    )
```

time: 248 us -> 59.2 us (0.24)
  local copies, waits for them, and re-layouts: 173 us -> 3.42 us
  Pallas kernels: 0 us -> 20.4 us
  waiting for transfers between devices: 13.8 us -> 0.72 us
  blocking collectives: 40.9 us -> 28.2 us
  matrix products: 7.59 us -> 0 us
  starting transfers between devices: 9.44 us -> 5.69 us
    gather x4 -> x0, local copies, waits for them, and re-layouts: 155 us -> none  [the longest x1 104 us: on_device(): columns_all = packed_cols[jnp.minimum(pair_order, packed_count - 1)]]
    psum x1 -> x0, blocking collectives: 40.9 us -> none  [on_device(): total = lax.psum(ordered, 'orb').astype(jnp.bfloat16)]
    all_to_all x0 -> x1, blocking collectives: none -> 28.2 us  [on_device(): lax.all_to_all(blocks, ('pair', 'orb'), 0, 0, axis_index_groups=groups, t...]
    pallas_call x0 -> x3, Pallas kernels: none -> 20.4 us  [the longest x1 8.02 us: select_stage(): pl.pallas_call(select_kernel, out_shape=jax.ShapeDtypeStruct((n_dest, 2,...]
    all_to_all x1 -> x0, waiting for transfers between devices: 13.8 us -> none  [on_device(): lax.all_to_all(total, 'pair', split_axis=1, concat_axis=0, tiled=True)]
    reshape x1 -> x4, local copies, waits for them, and re-layouts: 10.9 us -> 0.64 us  [the longest x2 0.32 us: places_of(): row = jnp.pad(row.reshape(n_pair, owned), pads).reshape(-1, 1, CHUNK)]
    all_to_all x1 -> x0, starting transfers between devices: 9.44 us -> none  [on_device(): lax.all_to_all(total, 'pair', split_axis=1, concat_axis=0, tiled=True)]
    dot_general x2 -> x0, matrix products: 7.59 us -> none  [the longest x1 6.01 us: on_device(): jnp.einsum('pi,kpj->kij', occ_rows, first_half, preferred_element_type=jn...]
  transfers between devices with their start and end apart: 1 -> 2, of which waited for: 1 -> 2; matrix products, arithmetic and copies ran while one was open for 0% -> 3% of each run, Pallas kernels for 0% -> 0%
where the time goes in v1:
time: 59.2 us; the launch traced here: 58.9 us
  blocking collectives  28.2 us (48%)
  Pallas kernels  20.4 us (34%)
  starting transfers between devices  5.69 us (10%)
  local copies, waits for them, and re-layouts  3.42 us (6%)
  waiting for transfers between devices  0.72 us (1%)
    all_to_all x1, blocking collectives, on_device(): lax.all_to_all(blocks, ('pair', 'orb'), 0, 0, axis_index_groups=groups, t...  28.2 us
    pallas_call x1, Pallas kernels, select_stage(): pl.pallas_call(select_kernel, out_shape=jax.ShapeDtypeStruct((n_dest, 2,...  8.02 us
    pallas_call x1, Pallas kernels, half_stage(): pl.pallas_call(half_kernel, grid=(np_ // block,), in_specs=[pl.BlockSpec(...  6.65 us
    pallas_call x1, Pallas kernels, final_stage(): pl.pallas_call(final_kernel, grid=(pl.cdiv(owned, block),), in_specs=[pl....  5.74 us
    ppermute x1, starting transfers between devices, on_device(): recv = lax.ppermute(send, 'orb', other_core)  3.31 us
    ppermute x1, starting transfers between devices, on_device(): other = lax.ppermute(own, 'orb', other_core)  2.38 us
  transfers between devices with their start and end apart: 2, of which 2 were waited for; matrix products, arithmetic and copies ran while one was open for 3% of the time, Pallas kernels for 0%

profile of v1, /device:TPU:1, one launch (start us, length us, event | category | flops | bytes accessed | tf_op | source)
XLA Modules:
  0.0 58.9 jit_solution(112756225418527645)
XLA Ops:
  0.0 0.0 copy-start
  0.0 0.0 copy-start.2
  0.0 0.0 copy-start.3
  0.0 1.1 %dynamic-slice_bitcast_fusion = bf16[200,306]{1,0:T(8,128)(2,1)S(1)} fusion(bf16[1224,200]{0,1:T(8,128)(2,1)} %param.6, s32[]{:T(128)S(6)} %select_n.61), kind=kLoop, calls=%fused_computation.2 | loop fusion | bytes 244804 | tf_op jit(solution)/shard_map/dynamic_slice | solution.py:192
  1.2 0.0 copy-start.1
  1.2 1.0 %copy-done.1 = bf16[1224,200]{0,1:T(8,128)(2,1)S(1)} copy-done((bf16[1224,200]{0,1:T(8,128)(2,1)S(1)}, bf16[1224,200]{0,1:T(8,128)(2,1)}, u32[]{:S(2)}) %copy-start.1) | copy-done | bytes 489624
  2.2 6.7 %half.1 = (f32[4,88,256]{2,1,0:T(8,128)S(1)}, bf16[4,88,256]{2,1,0:T(8,128)(2,1)S(1)}) custom-call(s32[1]{0:T(128)} %bitcast.core_ref, bf16[306,8,1224]{2,1,0:T(8,128)(2,1)} %bitcast.6, bf16[200,1224]{1,0:T(8,128)(2,1)S(1)} %bitcast.5, bf16[200,306]{1,0:T(8,128)(2,1)S(1)} %pad_maximum_fusion.ctp_ref), custom_call_target="tpu_custom_call" | custom-call | tf_op jit(solution)/shard_map/half/pallas_call | solution.py:129
  8.9 3.3 %collective-permute-start = (bf16[4,88,256]{2,1,0:T(8,128)(2,1)S(1)}, bf16[4,88,256]{2,1,0:T(8,128)(2,1)S(1)}, u32[]{:S(2)}, u32[]{:S(2)}) collective-permute-start(bf16[4,88,256]{2,1,0:T(8,128)(2,1)S(1)} %get-tuple-element.8), channel_id=1, source_target_pairs={{0,1},{1,0},{2,3},{3,2},{4,5},{5,4},{6,7},{7,6},{8,9},{9,8},{10,11... | collective-permute-start | bytes 540680 | tf_op jit(solution)/shard_map/ppermute | solution.py:208
  12.2 0.0 copy-done.2
  12.2 0.3 fusion
  12.5 0.2 reshape.18
  12.7 0.1 reshape.19.col_ref
  12.8 0.2 reshape.16
  13.1 0.1 reshape.17.row_ref
  13.2 0.1 collective-permute-done.recv_ref
  13.3 8.0 %select.17 = bf16[128,2,640]{2,1,0:T(2,128)(2,1)S(1)} custom-call(s32[16,1,1280]{2,1,0:T(1,128)S(1)} %reshape.17.row_ref, s32[16,1,1280]{2,1,0:T(1,128)S(1)} %reshape.19.col_ref, f32[4,88,256]{2,1,0:T(8,128)S(1)} %get-tuple-element.7.keep_ref, bf16[4,88,256]{2,1,0:T(8,128)(2,1)S(1)} %collective-permute-done.recv_ref), custom_call_target="tpu_custom_call" | custom-call | tf_op jit(solution)/shard_map/select/pallas_call | solution.py:160
  21.3 28.2 %all_to_all.5.own_ref = bf16[128,2,640]{2,1,0:T(2,128)(2,1)S(1)} all-to-all(bf16[128,2,640]{2,1,0:T(2,128)(2,1)S(1)} %select.17), channel_id=1, replica_groups={{0,2,4,6,8,10,12,14,16,18,20,22,24,26,28,30,32,34,36,38,40,42,44,46,48,..., dimensions={0} | all-to-all | bytes 655360 | tf_op jit(solution)/shard_map/all_to_all | solution.py:212
  49.5 2.4 %collective-permute-start.1 = (bf16[128,2,640]{2,1,0:T(2,128)(2,1)S(1)}, bf16[128,2,640]{2,1,0:T(2,128)(2,1)S(1)}, u32[]{:S(2)}, u32[]{:S(2)}) collective-permute-start(bf16[128,2,640]{2,1,0:T(2,128)(2,1)S(1)} %all_to_all.5.own_ref), channel_id=1, source_target_pairs={{0,1},{1,0},{2,3},{3,2},{4,5},{5,4},{6,7},{7,6},{8,9},{9,8},{10,11... | collective-permute-start | bytes 983048 | tf_op jit(solution)/shard_map/ppermute | solution.py:213
  51.9 0.0 copy-done.3
  51.9 0.0 copy-done
  51.9 0.6 %gather_fusion = bf16[16,256]{1,0:T(8,128)(2,1)S(1)} fusion(bf16[1224,256]{1,0:T(8,128)(2,1)S(1)} %copy-done, s32[1024]{0:T(1024)S(1)} %pad_clamp_fusion), kind=kCustom, calls=%fused_computation | custom fusion | bytes 16448 | tf_op jit(solution)/shard_map/gather | solution.py:214
  52.5 0.6 %collective-permute-done.1.other_ref = bf16[128,2,640]{2,1,0:T(2,128)(2,1)S(1)} collective-permute-done((bf16[128,2,640]{2,1,0:T(2,128)(2,1)S(1)}, bf16[128,2,640]{2,1,0:T(2,128)(2,1)S(1)}, u32[]{:S(2)}, u32[]{:S(2)}) %collective-permute-start.1) | collective-permute-done | bytes 327712 | tf_op jit(solution)/shard_map/ppermute | solution.py:213
  53.2 5.7 %final.1 = bf16[315,32,256]{2,1,0:T(8,128)(2,1)} custom-call(s32[1]{0:T(128)} %bitcast.core_ref, bf16[128,2,640]{2,1,0:T(2,128)(2,1)S(1)} %all_to_all.5.own_ref, bf16[128,2,640]{2,1,0:T(2,128)(2,1)S(1)} %collective-permute-done.1.other_ref, bf16[16,256]{1,0:T(8,128)(2,1)S(1)} %gather_fusion), custom_call_target="tpu_custom_call" | custom-call | tf_op jit(solution)/shard_map/final/pallas_call | solution.py:174
  (7 shorter events, 0.1 us)
Async XLA Ops:
  0.0 51.9 %copy-start = (bf16[1224,256]{1,0:T(8,128)(2,1)S(1)}, bf16[1224,256]{1,0:T(8,128)(2,1)}, u32[]{:S(2)}) copy-start(bf16[1224,256]{1,0:T(8,128)(2,1)} %param.7) | copy-start | bytes 1880068
  0.0 12.2 %copy-start.2 = (s32[20160]{0:T(1024)S(1)}, s32[20160]{0:T(1024)}, u32[]{:S(2)}) copy-start(s32[20160]{0:T(1024)} %param.9) | copy-start | bytes 241924
  0.0 51.9 %copy-start.3 = (s32[16]{0:T(128)S(1)}, s32[16]{0:T(128)}, u32[]{:S(2)}) copy-start(s32[16]{0:T(128)} %param.8) | copy-start | bytes 196
  1.2 1.0 %copy-start.1 = (bf16[1224,200]{0,1:T(8,128)(2,1)S(1)}, bf16[1224,200]{0,1:T(8,128)(2,1)}, u32[]{:S(2)}) copy-start(bf16[1224,200]{0,1:T(8,128)(2,1)} %param.6) | copy-start | bytes 1468804
  8.9 4.4 %collective-permute-start = (bf16[4,88,256]{2,1,0:T(8,128)(2,1)S(1)}, bf16[4,88,256]{2,1,0:T(8,128)(2,1)S(1)}, u32[]{:S(2)}, u32[]{:S(2)}) collective-permute-start(bf16[4,88,256]{2,1,0:T(8,128)(2,1)S(1)} %get-tuple-element.8), channel_id=1, source_target_pairs={{0,1},{1,0},{2,3},{3,2},{4,5},{5,4},{6,7},{7,6},{8,9},{9,8},{10,11... | collective-permute-start | bytes 540680 | tf_op jit(solution)/shard_map/ppermute | solution.py:208
  49.5 3.6 %collective-permute-start.1 = (bf16[128,2,640]{2,1,0:T(2,128)(2,1)S(1)}, bf16[128,2,640]{2,1,0:T(2,128)(2,1)S(1)}, u32[]{:S(2)}, u32[]{:S(2)}) collective-permute-start(bf16[128,2,640]{2,1,0:T(2,128)(2,1)S(1)} %all_to_all.5.own_ref), channel_id=1, source_target_pairs={{0,1},{1,0},{2,3},{3,2},{4,5},{5,4},{6,7},{7,6},{8,9},{9,8},{10,11... | collective-permute-start | bytes 983048 | tf_op jit(solution)/shard_map/ppermute | solution.py:213

commit v2 on v0

v2 whole, which is shorter than its diff:
```python
import jax
import jax.numpy as jnp
from jax import lax
from jax.experimental import pallas as pl
from jax.experimental.pallas import tpu as pltpu
from jax.sharding import PartitionSpec as P

NOCC = 200
COLS = 88
ROWS = 256
NPAIRS = NOCC * (NOCC + 1) // 2
KK = 8
HALF = 160
MSG = 10
CHUNK = 1280
LIMIT = 48 * 2**20


def fold(t):
    root = jnp.sqrt(8.0 * t.astype(jnp.float32) + 1.0)
    i = ((root - 1.0) * 0.5).astype(jnp.int32)
    i = jnp.where(i * (i + 1) > 2 * t, i - 1, i)
    i = jnp.where((i + 1) * (i + 2) <= 2 * t, i + 1, i)
    j = t - ((i * (i + 1)) >> 1)
    row = jnp.where(j < 88, i, jnp.where(j >= 113, j - 113, jnp.where(i >= 112, j + 112, j + 137)))
    col = jnp.where(j < 88, j, jnp.where((j >= 113) | (i >= 112), i - 112, i - 88))
    return row, jnp.where(t < NPAIRS, col, -1)


def half_kernel(orb_ref, ao_ref, ct_ref, keep_ref, send_ref, first_ref, ctp_ref):
    step = pl.program_id(0)
    block, kk, nq = ao_ref.shape
    np_ = ctp_ref.shape[1]
    for o in range(nq // np_):
        @pl.when((step == 0) & (orb_ref[0] == o))
        def _():
            ctp_ref[...] = ct_ref[:, o * np_:(o + 1) * np_]

    slab = ao_ref[...].reshape(block * kk, nq)
    first = lax.dot_general(slab, ct_ref[...], (((1,), (1,)), ((), ())), preferred_element_type=jnp.float32)
    at = pl.ds(pl.multiple_of(step * (block * kk), 8), block * kk)
    first_ref[0, at, :] = first[:, 0:128]
    first_ref[1, at, 0:NOCC - 128] = first[:, 128:NOCC]

    @pl.when(step == pl.num_programs(0) - 1)
    def _():
        lane = lax.broadcasted_iota(jnp.int32, (COLS, ROWS), 1)
        col = lax.broadcasted_iota(jnp.int32, (COLS, ROWS), 0)
        used = lax.broadcasted_iota(jnp.int32, (np_, 128), 1) < NOCC - 128
        ctp = ctp_ref[...]
        for k in range(kk):
            at = pl.ds(k, np_, stride=kk)
            right = jnp.where(used, first_ref[1, at, :], 0.0)
            fk = jnp.concatenate([first_ref[0, at, :], right], axis=1).astype(jnp.bfloat16)
            out = jnp.dot(ctp, fk, preferred_element_type=jnp.float32)
            o1 = out[0:88]
            o2 = out[112:200]
            o3 = jnp.concatenate([out[88:112], jnp.zeros((64, ROWS), jnp.float32)], axis=0)
            tri = jnp.where(lane >= col, o1, pltpu.roll(o2, ROWS - 113, 1))
            rest = jnp.where(lane < 225, pltpu.roll(o2, 112, 1), pltpu.roll(o3, 137, 1))
            keep_ref[k * COLS:(k + 1) * COLS, :] = jnp.where(lane < NOCC, tri, jnp.where(lane < 249, rest, 0.0))
        send_ref[...] = keep_ref[...].astype(jnp.bfloat16)


def half_stage(orb, slab, ct):
    np_, kk, nq = slab.shape
    block = 153
    kept = pl.BlockSpec((kk * COLS, ROWS), lambda i: (0, 0))
    return pl.pallas_call(
        half_kernel,
        grid=(np_ // block,),
        in_specs=[
            pl.BlockSpec(memory_space=pltpu.SMEM),
            pl.BlockSpec((block, kk, nq), lambda i: (i, 0, 0)),
            pl.BlockSpec((NOCC, nq), lambda i: (0, 0)),
        ],
        out_specs=[kept, kept],
        out_shape=[
            jax.ShapeDtypeStruct((kk * COLS, ROWS), jnp.float32),
            jax.ShapeDtypeStruct((kk * COLS, ROWS), jnp.bfloat16),
        ],
        scratch_shapes=[pltpu.VMEM((2, np_ * kk, 128), jnp.float32), pltpu.VMEM((NOCC, np_), jnp.bfloat16)],
        compiler_params=pltpu.CompilerParams(vmem_limit_bytes=LIMIT),
        name="half",
    )(orb, slab, ct)


def places_of(pair_order, core, n_pair):
    owned = pair_order.shape[0] // n_pair
    order = jnp.pad(pair_order.reshape(n_pair, owned), ((0, 0), (0, 2 * HALF - owned)), constant_values=NPAIRS)
    mine = jnp.where(core == 0, order[:, 0:HALF], order[:, HALF:2 * HALF])
    main = mine[:, 0:128].reshape(n_pair // 4, 512)
    left = mine[:, 128:HALF].reshape(n_pair // 4, 128)
    return jnp.concatenate([main, left], axis=1).reshape(-1, CHUNK)


def select_kernel(place_ref, keep_ref, recv_ref, vir_ref, out_ref, vbig_ref, tri_ref, row_ref, col_ref, stage_ref):
    line = lax.broadcasted_iota(jnp.int32, (256, 16), 0)
    s = lax.broadcasted_iota(jnp.int32, (256, 16), 1)
    hot = (s == ((line // 2) % 2) * 8 + line // 32).astype(jnp.bfloat16)
    vbig_ref[...] = jnp.dot(hot, vir_ref[...], preferred_element_type=jnp.float32).astype(jnp.bfloat16)
    tri_ref[...] = (keep_ref[...] + recv_ref[...].astype(jnp.float32)).astype(jnp.bfloat16)
    row, col = fold(place_ref[...])
    row_ref[...] = row
    col_ref[...] = col
    lane = lax.broadcasted_iota(jnp.int32, (KK, 128), 1)
    kpos = lax.broadcasted_iota(jnp.int32, (KK, 128), 0)
    first_col = lax.broadcasted_iota(jnp.int32, (8, CHUNK), 0)
    for ch in range(place_ref.shape[0]):
        row = row_ref[ch:ch + 1, :]
        col = col_ref[ch:ch + 1, :]
        hot = (lax.broadcasted_iota(jnp.int32, (ROWS, CHUNK), 0) == row).astype(jnp.bfloat16)
        picked = jnp.dot(tri_ref[...], hot, preferred_element_type=jnp.float32)
        accs = [jnp.zeros((8, CHUNK), jnp.float32)] * KK
        for v in range(COLS // 8):
            here = first_col + 8 * v == col
            accs = [jnp.where(here, picked[k * COLS + 8 * v:k * COLS + 8 * v + 8], a) for k, a in enumerate(accs)]
        vals = jnp.concatenate([jnp.sum(a, axis=0, keepdims=True) for a in accs], axis=0)
        for u in range(CHUNK // 640):
            left = vals[:, 640 * u + 512:640 * u + 640]
            turned = [left] + [pltpu.roll(left, 32 * s, 1) for s in (1, 2, 3)]
            for t in range(4):
                rest = turned[-t % 4]
                for j in (1, 2, 3):
                    rest = jnp.where(kpos // 2 == j, turned[(j - t) % 4], rest)
                rest = jnp.where(lane // 32 == kpos // 2, rest, 0.0)
                rest = rest[0:2] + rest[2:4] + rest[4:6] + rest[6:8]
                owner = 8 * ch + 4 * u + t
                for z in range(2):
                    at = (2 * owner + z) * MSG
                    stage_ref[at:at + 8, :] = vals[:, 640 * u + 128 * t:640 * u + 128 * (t + 1)]
                    stage_ref[at + 8:at + 10, :] = rest
    out_ref[...] = stage_ref[...].astype(jnp.bfloat16)


def select_stage(places, keep, recv, vir_rows):
    lines = places.shape[0] * (CHUNK // HALF) * 2 * MSG
    vmem = pl.BlockSpec(memory_space=pltpu.VMEM)
    return pl.pallas_call(
        select_kernel,
        out_shape=[
            jax.ShapeDtypeStruct((lines, 128), jnp.bfloat16),
            jax.ShapeDtypeStruct((256, 256), jnp.bfloat16),
        ],
        in_specs=[vmem] * 4,
        out_specs=[vmem, vmem],
        scratch_shapes=[
            pltpu.VMEM(keep.shape, jnp.bfloat16),
            pltpu.VMEM(places.shape, jnp.int32),
            pltpu.VMEM(places.shape, jnp.int32),
            pltpu.VMEM((lines, 128), jnp.float32),
        ],
        compiler_params=pltpu.CompilerParams(vmem_limit_bytes=LIMIT),
        name="select",
    )(places, keep, recv, vir_rows)


def final_kernel(share_ref, msg_ref, vbig_ref, *refs):
    out_ref, turned_ref, lines_ref = refs[-3:]
    step = pl.program_id(0)
    block = out_ref.shape[0]
    groups = turned_ref.shape[0]

    @pl.when(step == 0)
    def _():
        lines_ref[...] = msg_ref[...].astype(jnp.float32)
        for g in range(groups):
            at = 32 * MSG * g
            main = [lines_ref[pl.ds(at + k, 32, stride=MSG), :] for k in range(8)]
            turned_ref[g, 0:128, :] = jnp.concatenate(main, axis=0).T
            left = [lines_ref[pl.ds(at + k, 32, stride=MSG), :] for k in (8, 9)]
            left = jnp.concatenate(left, axis=0).T
            turned_ref[g, 128:HALF, :] = jnp.concatenate([left[32 * j:32 * (j + 1)] for j in range(4)], axis=1)

    lane = lax.broadcasted_iota(jnp.int32, (8, 256), 1)
    mask = (lane % 32) // 4 == lax.broadcasted_iota(jnp.int32, (8, 256), 0)
    at = pl.multiple_of(step * block, 8)
    for pair in range(groups // 2):
        parts = []
        for g in (2 * pair, 2 * pair + 1):
            rows = turned_ref[g, pl.ds(at, block), :]
            parts.append(jnp.where(mask[None], jnp.broadcast_to(rows[:, None, :], (block, 8, 256)), 0.0))
        lhs = jnp.concatenate(parts, axis=1).reshape(block * 16, 256).astype(jnp.bfloat16)
        res = jnp.dot(lhs, vbig_ref[...], preferred_element_type=jnp.float32)
        out_ref[:, 16 * pair:16 * (pair + 1), :] = res.reshape(block, 16, 256).astype(jnp.bfloat16)


def final_stage(share, msg, vbig, owned, into=None):
    block = 40
    steps = HALF // block
    held = [] if into is None else [into]
    return pl.pallas_call(
        final_kernel,
        grid_spec=pltpu.PrefetchScalarGridSpec(
            num_scalar_prefetch=1,
            grid=(steps,),
            in_specs=[
                pl.BlockSpec(msg.shape, lambda i, share: (0, 0)),
                pl.BlockSpec((256, 256), lambda i, share: (0, 0)),
            ] + [pl.BlockSpec(memory_space=pltpu.HBM)] * len(held),
            out_specs=pl.BlockSpec((block, 32, 256), lambda i, share: (share[0] * steps + i, 0, 0)),
            scratch_shapes=[
                pltpu.VMEM((4, HALF, 256), jnp.float32),
                pltpu.VMEM(msg.shape, jnp.float32),
            ],
        ),
        out_shape=jax.ShapeDtypeStruct((owned, 32, 256), jnp.bfloat16),
        input_output_aliases={3: 0} if held else {},
        compiler_params=pltpu.CompilerParams(vmem_limit_bytes=LIMIT),
        name="final",
    )(share, msg, vbig, *held)


def exchange(blocks, n_pair, n_orb):
    groups = [[p * n_orb + z * 2 + c for p in range(n_pair) for z in range(n_orb // 2)] for c in range(2)]
    packed = blocks.reshape(-1, MSG // 2, 2, 128)
    packed = lax.all_to_all(packed, ("pair", "orb"), 0, 0, axis_index_groups=groups, tiled=True)
    return packed.reshape(blocks.shape)


def on_device(ao_slab, occ_coef, vir_coef, tile_index, pair_order):
    n_pair = lax.axis_size("pair")
    n_orb = lax.axis_size("orb")
    orb = lax.axis_index("orb").astype(jnp.int32)
    core = orb & 1
    owned = pair_order.shape[0] // n_pair
    other_core = [(o, o ^ 1) for o in range(n_orb)]

    slab = jnp.transpose(ao_slab, (1, 0, 2))
    keep, send = half_stage(orb.reshape(1), slab, occ_coef.T)
    recv = lax.ppermute(send, "orb", other_core)
    places = places_of(pair_order, core, n_pair)
    blocks, vbig = select_stage(places, keep, recv, vir_coef[tile_index])
    own = exchange(blocks, n_pair, n_orb)
    other = lax.ppermute(own, "orb", other_core)
    mine = final_stage(core.reshape(1), own, vbig, owned)
    return final_stage((1 - core).reshape(1), other, vbig, owned, mine)


def solution(mesh):
    return jax.shard_map(
        on_device,
        mesh=mesh,
        in_specs=(P("pair", "orb", None), P(), P(None, "orb"), P(), P()),
        out_specs=P("pair", None, "orb"),
        check_vma=False,
    )
```

time: 248 us -> 52 us (0.21)
  local copies, waits for them, and re-layouts: 173 us -> 2.01 us
  Pallas kernels: 0 us -> 15.5 us
  waiting for transfers between devices: 13.8 us -> 0.22 us
  blocking collectives: 40.9 us -> 28.3 us
  matrix products: 7.59 us -> 0 us
  starting transfers between devices: 9.44 us -> 5.61 us
    gather x5 -> x1, local copies, waits for them, and re-layouts: 156 us -> 0.59 us  [on_device(): blocks, vbig = select_stage(places, keep, recv, vir_coef[tile_index])]
    psum x1 -> x0, blocking collectives: 40.9 us -> none  [on_device(): total = lax.psum(ordered, 'orb').astype(jnp.bfloat16)]
    all_to_all x0 -> x1, blocking collectives: none -> 28.3 us  [exchange(): lax.all_to_all(packed, ('pair', 'orb'), 0, 0, axis_index_groups=groups, t...]
    pallas_call x0 -> x4, Pallas kernels: none -> 15.5 us  [the longest x2 6.1 us: final_stage(): pl.pallas_call(final_kernel, grid_spec=pltpu.PrefetchScalarGridSpec(num_s...]
    all_to_all x1 -> x0, waiting for transfers between devices: 13.8 us -> none  [on_device(): lax.all_to_all(total, 'pair', split_axis=1, concat_axis=0, tiled=True)]
    reshape x1 -> x4, local copies, waits for them, and re-layouts: 10.9 us -> 0.29 us  [the longest x1 0.2 us: places_of(): pair_order.reshape(n_pair, owned)]
    all_to_all x1 -> x0, starting transfers between devices: 9.44 us -> none  [on_device(): lax.all_to_all(total, 'pair', split_axis=1, concat_axis=0, tiled=True)]
    dot_general x2 -> x0, matrix products: 7.59 us -> none  [the longest x1 6.01 us: on_device(): jnp.einsum('pi,kpj->kij', occ_rows, first_half, preferred_element_type=jn...]
  transfers between devices with their start and end apart: 1 -> 2, of which waited for: 1 -> 1; matrix products, arithmetic and copies ran while one was open for 0% -> 2% of each run, Pallas kernels for 0% -> 6%
where the time goes in v2:
time: 52 us; the launch traced here: 51.8 us
  blocking collectives  28.3 us (54%)
  Pallas kernels  15.5 us (30%)
  starting transfers between devices  5.61 us (11%)
  local copies, waits for them, and re-layouts  2.01 us (4%)
    all_to_all x1, blocking collectives, exchange(): lax.all_to_all(packed, ('pair', 'orb'), 0, 0, axis_index_groups=groups, t...  28.3 us
    pallas_call x2, Pallas kernels, final_stage(): pl.pallas_call(final_kernel, grid_spec=pltpu.PrefetchScalarGridSpec(num_s...  6.1 us
    pallas_call x1, Pallas kernels, half_stage(): pl.pallas_call(half_kernel, grid=(np_ // block,), in_specs=[pl.BlockSpec(...  5 us
    pallas_call x1, Pallas kernels, select_stage(): pl.pallas_call(select_kernel, out_shape=[jax.ShapeDtypeStruct((lines, 128...  4.36 us
    ppermute x1, starting transfers between devices, on_device(): recv = lax.ppermute(send, 'orb', other_core)  3.24 us
    ppermute x1, starting transfers between devices, on_device(): other = lax.ppermute(own, 'orb', other_core)  2.38 us
    unnamed x8, local copies, waits for them, and re-layouts  1.12 us
  transfers between devices with their start and end apart: 2, of which 1 were waited for; matrix products, arithmetic and copies ran while one was open for 2% of the time, Pallas kernels for 6%

profile of v2, /device:TPU:1, one launch (start us, length us, event | category | flops | bytes accessed | tf_op | source)
XLA Modules:
  0.0 51.8 jit_solution(2492546395007299414)
XLA Ops:
  0.0 0.0 copy-start
  0.0 0.0 copy-start.3
  0.0 0.0 copy-start.1
  0.0 1.1 %copy-done.1 = bf16[1224,200]{0,1:T(8,128)(2,1)S(1)} copy-done((bf16[1224,200]{0,1:T(8,128)(2,1)S(1)}, bf16[1224,200]{0,1:T(8,128)(2,1)}, u32[]{:S(2)}) %copy-start.1) | copy-done | bytes 489624
  1.1 0.0 copy-start.2
  1.1 5.0 %half.1 = (f32[704,256]{1,0:T(8,128)S(1)}, bf16[704,256]{1,0:T(8,128)(2,1)S(1)}) custom-call(s32[1]{0:T(128)} %bitcast.1.orb_ref, bf16[306,8,1224]{2,1,0:T(8,128)(2,1)} %bitcast.11, bf16[200,1224]{1,0:T(8,128)(2,1)S(1)} %bitcast.9), custom_call_target="tpu_custom_call" | custom-call | tf_op jit(solution)/shard_map/half/pallas_call | solution.py:69
  6.1 3.2 %collective-permute-start = (bf16[704,256]{1,0:T(8,128)(2,1)S(1)}, bf16[704,256]{1,0:T(8,128)(2,1)S(1)}, u32[]{:S(2)}, u32[]{:S(2)}) collective-permute-start(bf16[704,256]{1,0:T(8,128)(2,1)S(1)} %get-tuple-element.10), channel_id=1, source_target_pairs={{0,1},{1,0},{2,3},{3,2},{4,5},{5,4},{6,7},{7,6},{8,9},{9,8},{10,11... | collective-permute-start | bytes 1081352 | tf_op jit(solution)/shard_map/ppermute | solution.py:231
  9.4 0.0 copy-done.2
  9.4 0.2 reshape.28
  9.6 0.1 fusion
  9.7 0.1 reshape.30
  9.8 0.0 copy-done.3
  9.8 0.0 copy-done
  9.9 0.6 %gather_fusion = bf16[16,256]{1,0:T(8,128)(2,1)S(1)} fusion(bf16[1224,256]{1,0:T(8,128)(2,1)S(1)} %copy-done, s32[1024]{0:T(1024)S(1)} %pad_clamp_fusion), kind=kCustom, calls=%fused_computation | custom fusion | bytes 16448 | tf_op jit(solution)/shard_map/gather | solution.py:233
  10.4 0.2 collective-permute-done.recv_ref
  10.7 4.4 %select.2 = (bf16[1280,128]{1,0:T(8,128)(2,1)S(1)}, bf16[256,256]{1,0:T(8,128)(2,1)S(1)}) custom-call(s32[8,1280]{1,0:T(8,128)S(1)} %reshape.31.place_ref, f32[704,256]{1,0:T(8,128)S(1)} %get-tuple-element.9.keep_ref, bf16[704,256]{1,0:T(8,128)(2,1)S(1)} %collective-permute-done.recv_ref, bf16[16,256]{1,0:T(8,128)(2,1)S(1)} %gather_fusion), custom_call_target="tpu_custom_call" | custom-call | tf_op jit(solution)/shard_map/select/pallas_call | solution.py:139
  15.0 28.3 %all_to_all.5 = bf16[128,5,2,128]{3,2,1,0:T(2,128)(2,1)S(1)} all-to-all(bf16[128,5,2,128]{3,2,1,0:T(2,128)(2,1)S(1)} %bitcast.10), channel_id=1, replica_groups={{0,2,4,6,8,10,12,14,16,18,20,22,24,26,28,30,32,34,36,38,40,42,44,46,48,..., dimensions={0} | all-to-all | bytes 655360 | tf_op jit(solution)/shard_map/all_to_all | solution.py:217
  43.3 2.4 %collective-permute-start.1 = (bf16[1280,128]{1,0:T(8,128)(2,1)S(1)}, bf16[1280,128]{1,0:T(8,128)(2,1)S(1)}, u32[]{:S(2)}, u32[]{:S(2)}) collective-permute-start(bf16[1280,128]{1,0:T(8,128)(2,1)S(1)} %bitcast.7), channel_id=1, source_target_pairs={{0,1},{1,0},{2,3},{3,2},{4,5},{5,4},{6,7},{7,6},{8,9},{9,8},{10,11... | collective-permute-start | bytes 983048 | tf_op jit(solution)/shard_map/ppermute | solution.py:235
  45.7 3.0 %final.2.refs_0_ = bf16[315,32,256]{2,1,0:T(8,128)(2,1)} custom-call(s32[1]{0:T(128)} %bitcast.6.share_ref, bf16[1280,128]{1,0:T(8,128)(2,1)S(1)} %bitcast.8, bf16[256,256]{1,0:T(8,128)(2,1)S(1)} %get-tuple-element.12.vbig_ref), custom_call_target="tpu_custom_call" | custom-call | tf_op jit(solution)/shard_map/final/pallas_call | solution.py:192
  48.8 0.0 collective-permute-done.1.msg_ref
  48.8 3.1 %final.3 = bf16[315,32,256]{2,1,0:T(8,128)(2,1)} custom-call(s32[1]{0:T(128)} %bitcast.share_ref, bf16[1280,128]{1,0:T(8,128)(2,1)S(1)} %collective-permute-done.1.msg_ref, bf16[256,256]{1,0:T(8,128)(2,1)S(1)} %get-tuple-element.12.vbig_ref, bf16[315,32,256]{2,1,0:T(8,128)(2,1)} %final.2.refs_0_), custom_call_target="tpu_custom_call", output_to_operand_aliasing={{}: (3, {})} | custom-call | tf_op jit(solution)/shard_map/final/pallas_call | solution.py:192
  (7 shorter events, 0.0 us)
Async XLA Ops:
  0.0 9.8 %copy-start = (bf16[1224,256]{1,0:T(8,128)(2,1)S(1)}, bf16[1224,256]{1,0:T(8,128)(2,1)}, u32[]{:S(2)}) copy-start(bf16[1224,256]{1,0:T(8,128)(2,1)} %param.7) | copy-start | bytes 1880068
  0.0 9.8 %copy-start.3 = (s32[16]{0:T(128)S(1)}, s32[16]{0:T(128)}, u32[]{:S(2)}) copy-start(s32[16]{0:T(128)} %param.8) | copy-start | bytes 196
  0.0 1.1 %copy-start.1 = (bf16[1224,200]{0,1:T(8,128)(2,1)S(1)}, bf16[1224,200]{0,1:T(8,128)(2,1)}, u32[]{:S(2)}) copy-start(bf16[1224,200]{0,1:T(8,128)(2,1)} %param.6) | copy-start | bytes 1468804
  1.1 8.2 %copy-start.2 = (s32[20160]{0:T(1024)S(1)}, s32[20160]{0:T(1024)}, u32[]{:S(2)}) copy-start(s32[20160]{0:T(1024)} %param.9) | copy-start | bytes 241924
  6.1 4.5 %collective-permute-start = (bf16[704,256]{1,0:T(8,128)(2,1)S(1)}, bf16[704,256]{1,0:T(8,128)(2,1)S(1)}, u32[]{:S(2)}, u32[]{:S(2)}) collective-permute-start(bf16[704,256]{1,0:T(8,128)(2,1)S(1)} %get-tuple-element.10), channel_id=1, source_target_pairs={{0,1},{1,0},{2,3},{3,2},{4,5},{5,4},{6,7},{7,6},{8,9},{9,8},{10,11... | collective-permute-start | bytes 1081352 | tf_op jit(solution)/shard_map/ppermute | solution.py:231
  43.3 5.4 %collective-permute-start.1 = (bf16[1280,128]{1,0:T(8,128)(2,1)S(1)}, bf16[1280,128]{1,0:T(8,128)(2,1)S(1)}, u32[]{:S(2)}, u32[]{:S(2)}) collective-permute-start(bf16[1280,128]{1,0:T(8,128)(2,1)S(1)} %bitcast.7), channel_id=1, source_target_pairs={{0,1},{1,0},{2,3},{3,2},{4,5},{5,4},{6,7},{7,6},{8,9},{9,8},{10,11... | collective-permute-start | bytes 983048 | tf_op jit(solution)/shard_map/ppermute | solution.py:235

commit v3 on v2

--- a/solution.py
+++ b/solution.py
@@ -13,6 +13,7 @@
 HALF = 160
 MSG = 10
 CHUNK = 1280
+BLOCK = 40
 LIMIT = 48 * 2**20
 
 
@@ -156,55 +157,75 @@
 
 
 def final_kernel(share_ref, msg_ref, vbig_ref, *refs):
-    out_ref, turned_ref, lines_ref = refs[-3:]
-    step = pl.program_id(0)
-    block = out_ref.shape[0]
+    out_ref, held_ref, turned_ref, lines_ref, sem = refs[-5:]
     groups = turned_ref.shape[0]
-
-    @pl.when(step == 0)
-    def _():
-        lines_ref[...] = msg_ref[...].astype(jnp.float32)
-        for g in range(groups):
-            at = 32 * MSG * g
-            main = [lines_ref[pl.ds(at + k, 32, stride=MSG), :] for k in range(8)]
-            turned_ref[g, 0:128, :] = jnp.concatenate(main, axis=0).T
-            left = [lines_ref[pl.ds(at + k, 32, stride=MSG), :] for k in (8, 9)]
-            left = jnp.concatenate(left, axis=0).T
-            turned_ref[g, 128:HALF, :] = jnp.concatenate([left[32 * j:32 * (j + 1)] for j in range(4)], axis=1)
+    share = share_ref[0]
+    short = 2 * HALF - out_ref.shape[0]
+
+    lines_ref[...] = msg_ref[...].astype(jnp.float32)
+    for g in range(groups):
+        at = 32 * MSG * g
+        main = [lines_ref[pl.ds(at + k, 32, stride=MSG), :] for k in range(8)]
+        turned_ref[g, 0:128, :] = jnp.concatenate(main, axis=0).T
+        left = [lines_ref[pl.ds(at + k, 32, stride=MSG), :] for k in (8, 9)]
+        left = jnp.concatenate(left, axis=0).T
+        turned_ref[g, 128:HALF, :] = jnp.concatenate([left[32 * j:32 * (j + 1)] for j in range(4)], axis=1)
 
     lane = lax.broadcasted_iota(jnp.int32, (8, 256), 1)
     mask = (lane % 32) // 4 == lax.broadcasted_iota(jnp.int32, (8, 256), 0)
-    at = pl.multiple_of(step * block, 8)
-    for pair in range(groups // 2):
-        parts = []
-        for g in (2 * pair, 2 * pair + 1):
-            rows = turned_ref[g, pl.ds(at, block), :]
-            parts.append(jnp.where(mask[None], jnp.broadcast_to(rows[:, None, :], (block, 8, 256)), 0.0))
-        lhs = jnp.concatenate(parts, axis=1).reshape(block * 16, 256).astype(jnp.bfloat16)
-        res = jnp.dot(lhs, vbig_ref[...], preferred_element_type=jnp.float32)
-        out_ref[:, 16 * pair:16 * (pair + 1), :] = res.reshape(block, 16, 256).astype(jnp.bfloat16)
+
+    def copy(at, rows):
+        source = held_ref.at[pl.ds(at, rows)]
+        return pltpu.make_async_copy(source, out_ref.at[pl.ds(share * HALF + at, rows)], sem.at[at // BLOCK])
+
+    def each(act):
+        for at in range(0, HALF, BLOCK):
+            if at + BLOCK < HALF:
+                act(at, BLOCK)
+
+    def last(act):
+        at = HALF - BLOCK
+
+        @pl.when(share == 0)
+        def _():
+            act(at, BLOCK)
+
+        @pl.when(share != 0)
+        def _():
+            act(at, BLOCK - short)
+
+    for at in range(0, HALF, BLOCK):
+        for pair in range(groups // 2):
+            parts = []
+            for g in (2 * pair, 2 * pair + 1):
+                rows = turned_ref[g, at:at + BLOCK, :]
+                parts.append(jnp.where(mask[None], jnp.broadcast_to(rows[:, None, :], (BLOCK, 8, 256)), 0.0))
+            lhs = jnp.concatenate(parts, axis=1).reshape(BLOCK * 16, 256).astype(jnp.bfloat16)
+            res = jnp.dot(lhs, vbig_ref[...], preferred_element_type=jnp.float32)
+            res = res.reshape(BLOCK, 16, 256).astype(jnp.bfloat16)
+            held_ref[at:at + BLOCK, 16 * pair:16 * (pair + 1), :] = res
+        if at + BLOCK < HALF:
+            copy(at, BLOCK).start()
+    last(lambda at, rows: copy(at, rows).start())
+    each(lambda at, rows: copy(at, rows).wait())
+    last(lambda at, rows: copy(at, rows).wait())
 
 
 def final_stage(share, msg, vbig, owned, into=None):
-    block = 40
-    steps = HALF // block
     held = [] if into is None else [into]
+    vmem = pl.BlockSpec(memory_space=pltpu.VMEM)
+    hbm = pl.BlockSpec(memory_space=pltpu.HBM)
     return pl.pallas_call(
         final_kernel,
-        grid_spec=pltpu.PrefetchScalarGridSpec(
-            num_scalar_prefetch=1,
-            grid=(steps,),
-            in_specs=[
-                pl.BlockSpec(msg.shape, lambda i, share: (0, 0)),
-                pl.BlockSpec((256, 256), lambda i, share: (0, 0)),
-            ] + [pl.BlockSpec(memory_space=pltpu.HBM)] * len(held),
-            out_specs=pl.BlockSpec((block, 32, 256), lambda i, share: (share[0] * steps + i, 0, 0)),
-            scratch_shapes=[
-                pltpu.VMEM((4, HALF, 256), jnp.float32),
-                pltpu.VMEM(msg.shape, jnp.float32),
-            ],
-        ),
+        in_specs=[pl.BlockSpec(memory_space=pltpu.SMEM), vmem, vmem] + [hbm] * len(held),
+        out_specs=hbm,
         out_shape=jax.ShapeDtypeStruct((owned, 32, 256), jnp.bfloat16),
+        scratch_shapes=[
+            pltpu.VMEM((HALF, 32, 256), jnp.bfloat16),
+            pltpu.VMEM((4, HALF, 256), jnp.float32),
+            pltpu.VMEM(msg.shape, jnp.float32),
+            pltpu.SemaphoreType.DMA((HALF // BLOCK,)),
+        ],
         input_output_aliases={3: 0} if held else {},
         compiler_params=pltpu.CompilerParams(vmem_limit_bytes=LIMIT),
         name="final",
@@ -227,7 +248,7 @@
     other_core = [(o, o ^ 1) for o in range(n_orb)]
 
     slab = jnp.transpose(ao_slab, (1, 0, 2))
-    keep, send = half_stage(orb.reshape(1), slab, occ_coef.T)
+    keep, send = half_stage(orb.reshape(1), slab, pltpu.with_memory_space_constraint(occ_coef.T, pltpu.HBM))
     recv = lax.ppermute(send, "orb", other_core)
     places = places_of(pair_order, core, n_pair)
     blocks, vbig = select_stage(places, keep, recv, vir_coef[tile_index])

time: 52 us -> 48.9 us (0.940)
  Pallas kernels: 15.5 us -> 13.5 us
  local copies, waits for them, and re-layouts: 2.01 us -> 0.9 us
    pallas_call x2, Pallas kernels: 6.1 us -> 3.96 us  [final_stage(): pl.pallas_call(final_kernel, in_specs=[pl.BlockSpec(memory_space=pltpu.SM...]
    unnamed x8 -> x6, local copies, waits for them, and re-layouts: 1.12 us -> 0.01 us
  transfers between devices with their start and end apart: 2 -> 2, of which waited for: 1 -> 1; matrix products, arithmetic and copies ran while one was open for 2% -> 2% of each run, Pallas kernels for 6% -> 4%
where the time goes in v3:
time: 48.9 us; the launch traced here: 48.8 us
  blocking collectives  28.3 us (58%)
  Pallas kernels  13.5 us (28%)
  starting transfers between devices  5.59 us (11%)
  local copies, waits for them, and re-layouts  0.9 us (2%)
    all_to_all x1, blocking collectives, exchange(): lax.all_to_all(packed, ('pair', 'orb'), 0, 0, axis_index_groups=groups, t...  28.3 us
    pallas_call x1, Pallas kernels, half_stage(): pl.pallas_call(half_kernel, grid=(np_ // block,), in_specs=[pl.BlockSpec(...  5.18 us
    pallas_call x1, Pallas kernels, select_stage(): pl.pallas_call(select_kernel, out_shape=[jax.ShapeDtypeStruct((lines, 128...  4.36 us
    pallas_call x2, Pallas kernels, final_stage(): pl.pallas_call(final_kernel, in_specs=[pl.BlockSpec(memory_space=pltpu.SM...  3.96 us
    ppermute x1, starting transfers between devices, on_device(): recv = lax.ppermute(send, 'orb', other_core)  3.21 us
    ppermute x1, starting transfers between devices, on_device(): other = lax.ppermute(own, 'orb', other_core)  2.38 us
  transfers between devices with their start and end apart: 2, of which 1 were waited for; matrix products, arithmetic and copies ran while one was open for 2% of the time, Pallas kernels for 4%

profile of v3, /device:TPU:1, one launch (start us, length us, event | category | flops | bytes accessed | tf_op | source)
XLA Modules:
  0.0 48.8 jit_solution(3403129531929164353)
XLA Ops:
  0.0 0.0 copy-start
  0.0 0.0 copy-start.1
  0.0 0.0 copy-start.2
  0.0 5.2 %half.1 = (f32[704,256]{1,0:T(8,128)S(1)}, bf16[704,256]{1,0:T(8,128)(2,1)S(1)}) custom-call(s32[1]{0:T(128)} %bitcast.1.orb_ref, bf16[306,8,1224]{2,1,0:T(8,128)(2,1)} %bitcast.10, bf16[200,1224]{1,0:T(8,128)(2,1)} %bitcast.11), custom_call_target="tpu_custom_call" | custom-call | tf_op jit(solution)/shard_map/half/pallas_call | solution.py:70
  5.2 3.2 %collective-permute-start = (bf16[704,256]{1,0:T(8,128)(2,1)S(1)}, bf16[704,256]{1,0:T(8,128)(2,1)S(1)}, u32[]{:S(2)}, u32[]{:S(2)}) collective-permute-start(bf16[704,256]{1,0:T(8,128)(2,1)S(1)} %get-tuple-element.10), channel_id=1, source_target_pairs={{0,1},{1,0},{2,3},{3,2},{4,5},{5,4},{6,7},{7,6},{8,9},{9,8},{10,11... | collective-permute-start | bytes 1081352 | tf_op jit(solution)/shard_map/ppermute | solution.py:252
  8.4 0.0 copy-done.1
  8.4 0.2 reshape.28
  8.6 0.1 fusion
  8.7 0.1 reshape.30
  8.9 0.0 copy-done.2
  8.9 0.0 copy-done
  8.9 0.6 %gather_fusion = bf16[16,256]{1,0:T(8,128)(2,1)S(1)} fusion(bf16[1224,256]{1,0:T(8,128)(2,1)S(1)} %copy-done, s32[1024]{0:T(1024)S(1)} %pad_clamp_fusion), kind=kCustom, calls=%fused_computation | custom fusion | bytes 16448 | tf_op jit(solution)/shard_map/gather | solution.py:254
  9.5 0.2 collective-permute-done.recv_ref
  9.7 4.4 %select.2 = (bf16[1280,128]{1,0:T(8,128)(2,1)S(1)}, bf16[256,256]{1,0:T(8,128)(2,1)S(1)}) custom-call(s32[8,1280]{1,0:T(8,128)S(1)} %reshape.31.place_ref, f32[704,256]{1,0:T(8,128)S(1)} %get-tuple-element.9.keep_ref, bf16[704,256]{1,0:T(8,128)(2,1)S(1)} %collective-permute-done.recv_ref, bf16[16,256]{1,0:T(8,128)(2,1)S(1)} %gather_fusion), custom_call_target="tpu_custom_call" | custom-call | tf_op jit(solution)/shard_map/select/pallas_call | solution.py:140
  14.1 28.3 %all_to_all.5 = bf16[128,5,2,128]{3,2,1,0:T(2,128)(2,1)S(1)} all-to-all(bf16[128,5,2,128]{3,2,1,0:T(2,128)(2,1)S(1)} %bitcast.9), channel_id=1, replica_groups={{0,2,4,6,8,10,12,14,16,18,20,22,24,26,28,30,32,34,36,38,40,42,44,46,48,..., dimensions={0} | all-to-all | bytes 655360 | tf_op jit(solution)/shard_map/all_to_all | solution.py:238
  42.4 2.4 %collective-permute-start.1 = (bf16[1280,128]{1,0:T(8,128)(2,1)S(1)}, bf16[1280,128]{1,0:T(8,128)(2,1)S(1)}, u32[]{:S(2)}, u32[]{:S(2)}) collective-permute-start(bf16[1280,128]{1,0:T(8,128)(2,1)S(1)} %bitcast.7), channel_id=1, source_target_pairs={{0,1},{1,0},{2,3},{3,2},{4,5},{5,4},{6,7},{7,6},{8,9},{9,8},{10,11... | collective-permute-start | bytes 983048 | tf_op jit(solution)/shard_map/ppermute | solution.py:256
  44.8 2.0 %final.2.refs_0_ = bf16[315,32,256]{2,1,0:T(8,128)(2,1)} custom-call(s32[1]{0:T(128)} %bitcast.6.share_ref, bf16[1280,128]{1,0:T(8,128)(2,1)S(1)} %bitcast.8, bf16[256,256]{1,0:T(8,128)(2,1)S(1)} %get-tuple-element.12.vbig_ref), custom_call_target="tpu_custom_call" | custom-call | tf_op jit(solution)/shard_map/final/pallas_call | solution.py:218
  46.7 0.0 collective-permute-done.1.msg_ref
  46.8 2.0 %final.3 = bf16[315,32,256]{2,1,0:T(8,128)(2,1)} custom-call(s32[1]{0:T(128)} %bitcast.share_ref, bf16[1280,128]{1,0:T(8,128)(2,1)S(1)} %collective-permute-done.1.msg_ref, bf16[256,256]{1,0:T(8,128)(2,1)S(1)} %get-tuple-element.12.vbig_ref, bf16[315,32,256]{2,1,0:T(8,128)(2,1)} %final.2.refs_0_), custom_call_target="tpu_custom_call", output_to_operand_aliasing={{}: (3, {})} | custom-call | tf_op jit(solution)/shard_map/final/pallas_call | solution.py:218
  (7 shorter events, 0.0 us)
Async XLA Ops:
  0.0 8.9 %copy-start = (bf16[1224,256]{1,0:T(8,128)(2,1)S(1)}, bf16[1224,256]{1,0:T(8,128)(2,1)}, u32[]{:S(2)}) copy-start(bf16[1224,256]{1,0:T(8,128)(2,1)} %param.7) | copy-start | bytes 1880068
  0.0 8.4 %copy-start.1 = (s32[20160]{0:T(1024)S(1)}, s32[20160]{0:T(1024)}, u32[]{:S(2)}) copy-start(s32[20160]{0:T(1024)} %param.9) | copy-start | bytes 241924
  0.0 8.9 %copy-start.2 = (s32[16]{0:T(128)S(1)}, s32[16]{0:T(128)}, u32[]{:S(2)}) copy-start(s32[16]{0:T(128)} %param.8) | copy-start | bytes 196
  5.2 4.5 %collective-permute-start = (bf16[704,256]{1,0:T(8,128)(2,1)S(1)}, bf16[704,256]{1,0:T(8,128)(2,1)S(1)}, u32[]{:S(2)}, u32[]{:S(2)}) collective-permute-start(bf16[704,256]{1,0:T(8,128)(2,1)S(1)} %get-tuple-element.10), channel_id=1, source_target_pairs={{0,1},{1,0},{2,3},{3,2},{4,5},{5,4},{6,7},{7,6},{8,9},{9,8},{10,11... | collective-permute-start | bytes 1081352 | tf_op jit(solution)/shard_map/ppermute | solution.py:252
  42.4 4.4 %collective-permute-start.1 = (bf16[1280,128]{1,0:T(8,128)(2,1)S(1)}, bf16[1280,128]{1,0:T(8,128)(2,1)S(1)}, u32[]{:S(2)}, u32[]{:S(2)}) collective-permute-start(bf16[1280,128]{1,0:T(8,128)(2,1)S(1)} %bitcast.7), channel_id=1, source_target_pairs={{0,1},{1,0},{2,3},{3,2},{4,5},{5,4},{6,7},{7,6},{8,9},{9,8},{10,11... | collective-permute-start | bytes 983048 | tf_op jit(solution)/shard_map/ppermute | solution.py:256

commit v4 on v3

--- a/solution.py
+++ b/solution.py
@@ -6,7 +6,7 @@
 from jax.sharding import PartitionSpec as P
 
 NOCC = 200
-COLS = 88
+COLS = 80
 ROWS = 256
 NPAIRS = NOCC * (NOCC + 1) // 2
 KK = 8
@@ -23,8 +23,12 @@
     i = jnp.where(i * (i + 1) > 2 * t, i - 1, i)
     i = jnp.where((i + 1) * (i + 2) <= 2 * t, i + 1, i)
     j = t - ((i * (i + 1)) >> 1)
-    row = jnp.where(j < 88, i, jnp.where(j >= 113, j - 113, jnp.where(i >= 112, j + 112, j + 137)))
-    col = jnp.where(j < 88, j, jnp.where((j >= 113) | (i >= 112), i - 112, i - 88))
+    low = i < 120
+    row = jnp.where(j < 95, j + 161, jnp.where(j < 110, j + 146, j + 131))
+    row = jnp.where(low, row, j + 120)
+    row = jnp.where(j < 80, i, jnp.where(j > 120, j - 121, row))
+    col = jnp.where(j < 95, i - 80, jnp.where(j < 110, i - 55, i - 45))
+    col = jnp.where(j < 80, j, jnp.where(low, col, i - 120))
     return row, jnp.where(t < NPAIRS, col, -1)
 
 
@@ -45,21 +49,22 @@
 
     @pl.when(step == pl.num_programs(0) - 1)
     def _():
-        lane = lax.broadcasted_iota(jnp.int32, (COLS, ROWS), 1)
-        col = lax.broadcasted_iota(jnp.int32, (COLS, ROWS), 0)
-        used = lax.broadcasted_iota(jnp.int32, (np_, 128), 1) < NOCC - 128
+        lane = lax.broadcasted_iota(jnp.int32, (COLS, 128), 1)
+        col = lax.broadcasted_iota(jnp.int32, (COLS, 128), 0)
         ctp = ctp_ref[...]
         for k in range(kk):
             at = pl.ds(k, np_, stride=kk)
-            right = jnp.where(used, first_ref[1, at, :], 0.0)
-            fk = jnp.concatenate([first_ref[0, at, :], right], axis=1).astype(jnp.bfloat16)
+            fk = jnp.concatenate([first_ref[0, at, :], first_ref[1, at, :]], axis=1).astype(jnp.bfloat16)
             out = jnp.dot(ctp, fk, preferred_element_type=jnp.float32)
-            o1 = out[0:88]
-            o2 = out[112:200]
-            o3 = jnp.concatenate([out[88:112], jnp.zeros((64, ROWS), jnp.float32)], axis=0)
-            tri = jnp.where(lane >= col, o1, pltpu.roll(o2, ROWS - 113, 1))
-            rest = jnp.where(lane < 225, pltpu.roll(o2, 112, 1), pltpu.roll(o3, 137, 1))
-            keep_ref[k * COLS:(k + 1) * COLS, :] = jnp.where(lane < NOCC, tri, jnp.where(lane < 249, rest, 0.0))
+            a, b = out[:, 0:128], out[:, 128:256]
+            wrap = jnp.where(lane < 7, pltpu.roll(a[120:200], 7, 1), pltpu.roll(b[120:200], 7, 1))
+            mid = jnp.concatenate([a[80:120], a[95:120], a[110:120], jnp.zeros((5, 128), jnp.float32)], axis=0)
+            low = jnp.where(col < 65, pltpu.roll(mid, 18, 1), pltpu.roll(mid, 3, 1))
+            low = jnp.where(col < 40, pltpu.roll(mid, 33, 1), low)
+            rest = jnp.where(lane < 113, pltpu.roll(a[120:200], 120, 1), low)
+            rows = pl.ds(k * COLS, COLS)
+            keep_ref[rows, 0:128] = jnp.where(lane >= col, a[0:80], wrap)
+            keep_ref[rows, 128:256] = jnp.where(lane < 72, b[0:80], rest)
         send_ref[...] = keep_ref[...].astype(jnp.bfloat16)
 
 

time: 48.9 us -> 48.4 us (0.990)
  Pallas kernels: 13.5 us -> 13 us
where the time goes in v4:
time: 48.4 us; the launch traced here: 48.3 us
  blocking collectives  28.3 us (58%)
  Pallas kernels  13 us (27%)
  starting transfers between devices  5.6 us (12%)
  local copies, waits for them, and re-layouts  0.9 us (2%)
    all_to_all x1, blocking collectives, exchange(): lax.all_to_all(packed, ('pair', 'orb'), 0, 0, axis_index_groups=groups, t...  28.3 us
    pallas_call x1, Pallas kernels, half_stage(): pl.pallas_call(half_kernel, grid=(np_ // block,), in_specs=[pl.BlockSpec(...  5.14 us
    pallas_call x2, Pallas kernels, final_stage(): pl.pallas_call(final_kernel, in_specs=[pl.BlockSpec(memory_space=pltpu.SM...  3.97 us
    pallas_call x1, Pallas kernels, select_stage(): pl.pallas_call(select_kernel, out_shape=[jax.ShapeDtypeStruct((lines, 128...  3.94 us
    ppermute x1, starting transfers between devices, on_device(): recv = lax.ppermute(send, 'orb', other_core)  3.22 us
    ppermute x1, starting transfers between devices, on_device(): other = lax.ppermute(own, 'orb', other_core)  2.38 us
  transfers between devices with their start and end apart: 2, of which 1 were waited for; matrix products, arithmetic and copies ran while one was open for 2% of the time, Pallas kernels for 4%

profile of v4, /device:TPU:1, one launch (start us, length us, event | category | flops | bytes accessed | tf_op | source)
XLA Modules:
  0.0 48.3 jit_solution(13723147224060237961)
XLA Ops:
  0.0 0.0 copy-start
  0.0 0.0 copy-start.1
  0.0 0.0 copy-start.2
  0.0 5.1 %half.1 = (f32[640,256]{1,0:T(8,128)S(1)}, bf16[640,256]{1,0:T(8,128)(2,1)S(1)}) custom-call(s32[1]{0:T(128)} %bitcast.1.orb_ref, bf16[306,8,1224]{2,1,0:T(8,128)(2,1)} %bitcast.10, bf16[200,1224]{1,0:T(8,128)(2,1)} %bitcast.11), custom_call_target="tpu_custom_call" | custom-call | tf_op jit(solution)/shard_map/half/pallas_call | solution.py:75
  5.2 3.2 %collective-permute-start = (bf16[640,256]{1,0:T(8,128)(2,1)S(1)}, bf16[640,256]{1,0:T(8,128)(2,1)S(1)}, u32[]{:S(2)}, u32[]{:S(2)}) collective-permute-start(bf16[640,256]{1,0:T(8,128)(2,1)S(1)} %get-tuple-element.10), channel_id=1, source_target_pairs={{0,1},{1,0},{2,3},{3,2},{4,5},{5,4},{6,7},{7,6},{8,9},{9,8},{10,11... | collective-permute-start | bytes 983048 | tf_op jit(solution)/shard_map/ppermute | solution.py:257
  8.4 0.0 copy-done.1
  8.4 0.2 reshape.28
  8.6 0.1 fusion
  8.7 0.1 reshape.30
  8.8 0.0 copy-done.2
  8.9 0.0 copy-done
  8.9 0.6 %gather_fusion = bf16[16,256]{1,0:T(8,128)(2,1)S(1)} fusion(bf16[1224,256]{1,0:T(8,128)(2,1)S(1)} %copy-done, s32[1024]{0:T(1024)S(1)} %pad_clamp_fusion), kind=kCustom, calls=%fused_computation | custom fusion | bytes 16448 | tf_op jit(solution)/shard_map/gather | solution.py:259
  9.5 0.2 collective-permute-done.recv_ref
  9.6 3.9 %select.2 = (bf16[1280,128]{1,0:T(8,128)(2,1)S(1)}, bf16[256,256]{1,0:T(8,128)(2,1)S(1)}) custom-call(s32[8,1280]{1,0:T(8,128)S(1)} %reshape.31.place_ref, f32[640,256]{1,0:T(8,128)S(1)} %get-tuple-element.9.keep_ref, bf16[640,256]{1,0:T(8,128)(2,1)S(1)} %collective-permute-done.recv_ref, bf16[16,256]{1,0:T(8,128)(2,1)S(1)} %gather_fusion), custom_call_target="tpu_custom_call" | custom-call | tf_op jit(solution)/shard_map/select/pallas_call | solution.py:145
  13.6 28.3 %all_to_all.5 = bf16[128,5,2,128]{3,2,1,0:T(2,128)(2,1)S(1)} all-to-all(bf16[128,5,2,128]{3,2,1,0:T(2,128)(2,1)S(1)} %bitcast.9), channel_id=1, replica_groups={{0,2,4,6,8,10,12,14,16,18,20,22,24,26,28,30,32,34,36,38,40,42,44,46,48,..., dimensions={0} | all-to-all | bytes 655360 | tf_op jit(solution)/shard_map/all_to_all | solution.py:243
  41.9 2.4 %collective-permute-start.1 = (bf16[1280,128]{1,0:T(8,128)(2,1)S(1)}, bf16[1280,128]{1,0:T(8,128)(2,1)S(1)}, u32[]{:S(2)}, u32[]{:S(2)}) collective-permute-start(bf16[1280,128]{1,0:T(8,128)(2,1)S(1)} %bitcast.7), channel_id=1, source_target_pairs={{0,1},{1,0},{2,3},{3,2},{4,5},{5,4},{6,7},{7,6},{8,9},{9,8},{10,11... | collective-permute-start | bytes 983048 | tf_op jit(solution)/shard_map/ppermute | solution.py:261
  44.3 2.0 %final.2.refs_0_ = bf16[315,32,256]{2,1,0:T(8,128)(2,1)} custom-call(s32[1]{0:T(128)} %bitcast.6.share_ref, bf16[1280,128]{1,0:T(8,128)(2,1)S(1)} %bitcast.8, bf16[256,256]{1,0:T(8,128)(2,1)S(1)} %get-tuple-element.12.vbig_ref), custom_call_target="tpu_custom_call" | custom-call | tf_op jit(solution)/shard_map/final/pallas_call | solution.py:223
  46.3 0.0 collective-permute-done.1.msg_ref
  46.3 2.0 %final.3 = bf16[315,32,256]{2,1,0:T(8,128)(2,1)} custom-call(s32[1]{0:T(128)} %bitcast.share_ref, bf16[1280,128]{1,0:T(8,128)(2,1)S(1)} %collective-permute-done.1.msg_ref, bf16[256,256]{1,0:T(8,128)(2,1)S(1)} %get-tuple-element.12.vbig_ref, bf16[315,32,256]{2,1,0:T(8,128)(2,1)} %final.2.refs_0_), custom_call_target="tpu_custom_call", output_to_operand_aliasing={{}: (3, {})} | custom-call | tf_op jit(solution)/shard_map/final/pallas_call | solution.py:223
  (7 shorter events, 0.0 us)
Async XLA Ops:
  0.0 8.9 %copy-start = (bf16[1224,256]{1,0:T(8,128)(2,1)S(1)}, bf16[1224,256]{1,0:T(8,128)(2,1)}, u32[]{:S(2)}) copy-start(bf16[1224,256]{1,0:T(8,128)(2,1)} %param.7) | copy-start | bytes 1880068
  0.0 8.4 %copy-start.1 = (s32[20160]{0:T(1024)S(1)}, s32[20160]{0:T(1024)}, u32[]{:S(2)}) copy-start(s32[20160]{0:T(1024)} %param.9) | copy-start | bytes 241924
  0.0 8.8 %copy-start.2 = (s32[16]{0:T(128)S(1)}, s32[16]{0:T(128)}, u32[]{:S(2)}) copy-start(s32[16]{0:T(128)} %param.8) | copy-start | bytes 196
  5.2 4.5 %collective-permute-start = (bf16[640,256]{1,0:T(8,128)(2,1)S(1)}, bf16[640,256]{1,0:T(8,128)(2,1)S(1)}, u32[]{:S(2)}, u32[]{:S(2)}) collective-permute-start(bf16[640,256]{1,0:T(8,128)(2,1)S(1)} %get-tuple-element.10), channel_id=1, source_target_pairs={{0,1},{1,0},{2,3},{3,2},{4,5},{5,4},{6,7},{7,6},{8,9},{9,8},{10,11... | collective-permute-start | bytes 983048 | tf_op jit(solution)/shard_map/ppermute | solution.py:257
  41.9 4.4 %collective-permute-start.1 = (bf16[1280,128]{1,0:T(8,128)(2,1)S(1)}, bf16[1280,128]{1,0:T(8,128)(2,1)S(1)}, u32[]{:S(2)}, u32[]{:S(2)}) collective-permute-start(bf16[1280,128]{1,0:T(8,128)(2,1)S(1)} %bitcast.7), channel_id=1, source_target_pairs={{0,1},{1,0},{2,3},{3,2},{4,5},{5,4},{6,7},{7,6},{8,9},{9,8},{10,11... | collective-permute-start | bytes 983048 | tf_op jit(solution)/shard_map/ppermute | solution.py:261

commit v5 on v4

--- a/solution.py
+++ b/solution.py
@@ -12,8 +12,9 @@
 KK = 8
 HALF = 160
 MSG = 10
-CHUNK = 1280
+CHUNK = 2560
 BLOCK = 40
+EARLY = 80
 LIMIT = 48 * 2**20
 
 
@@ -115,7 +116,8 @@
     for ch in range(place_ref.shape[0]):
         row = row_ref[ch:ch + 1, :]
         col = col_ref[ch:ch + 1, :]
-        hot = (lax.broadcasted_iota(jnp.int32, (ROWS, CHUNK), 0) == row).astype(jnp.bfloat16)
+        same = lax.broadcasted_iota(jnp.int16, (ROWS, CHUNK), 0) == row.astype(jnp.int16)
+        hot = jnp.where(same, jnp.ones((), jnp.bfloat16), jnp.zeros((), jnp.bfloat16))
         picked = jnp.dot(tri_ref[...], hot, preferred_element_type=jnp.float32)
         accs = [jnp.zeros((8, CHUNK), jnp.float32)] * KK
         for v in range(COLS // 8):
@@ -131,7 +133,7 @@
                     rest = jnp.where(kpos // 2 == j, turned[(j - t) % 4], rest)
                 rest = jnp.where(lane // 32 == kpos // 2, rest, 0.0)
                 rest = rest[0:2] + rest[2:4] + rest[4:6] + rest[6:8]
-                owner = 8 * ch + 4 * u + t
+                owner = CHUNK // HALF * ch + 4 * u + t
                 for z in range(2):
                     at = (2 * owner + z) * MSG
                     stage_ref[at:at + 8, :] = vals[:, 640 * u + 128 * t:640 * u + 128 * (t + 1)]
@@ -161,14 +163,9 @@
     )(places, keep, recv, vir_rows)
 
 
-def final_kernel(share_ref, msg_ref, vbig_ref, *refs):
-    out_ref, held_ref, turned_ref, lines_ref, sem = refs[-5:]
-    groups = turned_ref.shape[0]
-    share = share_ref[0]
-    short = 2 * HALF - out_ref.shape[0]
-
+def turn(msg_ref, lines_ref, turned_ref):
     lines_ref[...] = msg_ref[...].astype(jnp.float32)
-    for g in range(groups):
+    for g in range(turned_ref.shape[0]):
         at = 32 * MSG * g
         main = [lines_ref[pl.ds(at + k, 32, stride=MSG), :] for k in range(8)]
         turned_ref[g, 0:128, :] = jnp.concatenate(main, axis=0).T
@@ -176,65 +173,110 @@
         left = jnp.concatenate(left, axis=0).T
         turned_ref[g, 128:HALF, :] = jnp.concatenate([left[32 * j:32 * (j + 1)] for j in range(4)], axis=1)
 
+
+def quarter(turned_ref, vbig_ref, at, into_ref, to):
     lane = lax.broadcasted_iota(jnp.int32, (8, 256), 1)
     mask = (lane % 32) // 4 == lax.broadcasted_iota(jnp.int32, (8, 256), 0)
-
-    def copy(at, rows):
-        source = held_ref.at[pl.ds(at, rows)]
-        return pltpu.make_async_copy(source, out_ref.at[pl.ds(share * HALF + at, rows)], sem.at[at // BLOCK])
-
-    def each(act):
-        for at in range(0, HALF, BLOCK):
-            if at + BLOCK < HALF:
-                act(at, BLOCK)
-
-    def last(act):
-        at = HALF - BLOCK
-
-        @pl.when(share == 0)
-        def _():
-            act(at, BLOCK)
-
-        @pl.when(share != 0)
-        def _():
-            act(at, BLOCK - short)
-
+    for pair in range(turned_ref.shape[0] // 2):
+        parts = []
+        for g in (2 * pair, 2 * pair + 1):
+            rows = turned_ref[g, at:at + BLOCK, :]
+            parts.append(jnp.where(mask[None], jnp.broadcast_to(rows[:, None, :], (BLOCK, 8, 256)), 0.0))
+        lhs = jnp.concatenate(parts, axis=1).reshape(BLOCK * 16, 256).astype(jnp.bfloat16)
+        res = jnp.dot(lhs, vbig_ref[...], preferred_element_type=jnp.float32)
+        res = res.reshape(BLOCK, 16, 256).astype(jnp.bfloat16)
+        into_ref[to:to + BLOCK, 16 * pair:16 * (pair + 1), :] = res
+
+
+def cut(share, act, source_ref, begin, rows, out_ref, at, sem):
+    short = 2 * HALF - out_ref.shape[0]
+
+    def copy(n):
+        return pltpu.make_async_copy(source_ref.at[pl.ds(begin, n)], out_ref.at[pl.ds(share * HALF + at, n)], sem)
+
+    @pl.when(share == 0)
+    def _():
+        act(copy(rows))
+
+    @pl.when(share != 0)
+    def _():
+        act(copy(rows - short))
+
+
+def own_kernel(share_ref, msg_ref, vbig_ref, out_ref, rest_ref, held_ref, turned_ref, lines_ref, sem):
+    share = share_ref[0]
+
+    def copy(at):
+        source = held_ref.at[pl.ds(at, BLOCK)]
+        return pltpu.make_async_copy(source, out_ref.at[pl.ds(share * HALF + at, BLOCK)], sem.at[at // BLOCK])
+
+    turn(msg_ref, lines_ref, turned_ref)
+    for at in range(0, EARLY, BLOCK):
+        quarter(turned_ref, vbig_ref, at, held_ref, at)
+        copy(at).start()
+    for at in range(EARLY, HALF, BLOCK):
+        quarter(turned_ref, vbig_ref, at, rest_ref, at - EARLY)
+    for at in range(0, EARLY, BLOCK):
+        copy(at).wait()
+
+
+def other_kernel(share_ref, msg_ref, vbig_ref, rest_ref, into_ref, out_ref, held_ref, turned_ref, lines_ref, sem):
+    del into_ref
+    share = share_ref[0]
+    end = HALF - BLOCK
+    late = HALF // BLOCK
+
+    def copy(at):
+        source = held_ref.at[pl.ds(at, BLOCK)]
+        return pltpu.make_async_copy(source, out_ref.at[pl.ds(share * HALF + at, BLOCK)], sem.at[at // BLOCK])
+
+    cut(1 - share, lambda c: c.start(), rest_ref, 0, HALF - EARLY, out_ref, EARLY, sem.at[late])
+    turn(msg_ref, lines_ref, turned_ref)
     for at in range(0, HALF, BLOCK):
-        for pair in range(groups // 2):
-            parts = []
-            for g in (2 * pair, 2 * pair + 1):
-                rows = turned_ref[g, at:at + BLOCK, :]
-                parts.append(jnp.where(mask[None], jnp.broadcast_to(rows[:, None, :], (BLOCK, 8, 256)), 0.0))
-            lhs = jnp.concatenate(parts, axis=1).reshape(BLOCK * 16, 256).astype(jnp.bfloat16)
-            res = jnp.dot(lhs, vbig_ref[...], preferred_element_type=jnp.float32)
-            res = res.reshape(BLOCK, 16, 256).astype(jnp.bfloat16)
-            held_ref[at:at + BLOCK, 16 * pair:16 * (pair + 1), :] = res
-        if at + BLOCK < HALF:
-            copy(at, BLOCK).start()
-    last(lambda at, rows: copy(at, rows).start())
-    each(lambda at, rows: copy(at, rows).wait())
-    last(lambda at, rows: copy(at, rows).wait())
-
-
-def final_stage(share, msg, vbig, owned, into=None):
-    held = [] if into is None else [into]
+        quarter(turned_ref, vbig_ref, at, held_ref, at)
+        if at < end:
+            copy(at).start()
+    cut(share, lambda c: c.start(), held_ref, end, BLOCK, out_ref, end, sem.at[end // BLOCK])
+    cut(1 - share, lambda c: c.wait(), rest_ref, 0, HALF - EARLY, out_ref, EARLY, sem.at[late])
+    for at in range(0, end, BLOCK):
+        copy(at).wait()
+    cut(share, lambda c: c.wait(), held_ref, end, BLOCK, out_ref, end, sem.at[end // BLOCK])
+
+
+def final_stage(core, own, other, vbig, owned):
+    smem = pl.BlockSpec(memory_space=pltpu.SMEM)
     vmem = pl.BlockSpec(memory_space=pltpu.VMEM)
     hbm = pl.BlockSpec(memory_space=pltpu.HBM)
+    whole = jax.ShapeDtypeStruct((owned, 32, 256), jnp.bfloat16)
+    params = pltpu.CompilerParams(vmem_limit_bytes=LIMIT)
+
+    def scratch(rows):
+        return [
+            pltpu.VMEM((rows, 32, 256), jnp.bfloat16),
+            pltpu.VMEM((4, HALF, 256), jnp.float32),
+            pltpu.VMEM(own.shape, jnp.float32),
+            pltpu.SemaphoreType.DMA((HALF // BLOCK + 1,)),
+        ]
+
+    out, rest = pl.pallas_call(
+        own_kernel,
+        in_specs=[smem, vmem, vmem],
+        out_specs=[hbm, vmem],
+        out_shape=[whole, jax.ShapeDtypeStruct((HALF - EARLY, 32, 256), jnp.bfloat16)],
+        scratch_shapes=scratch(EARLY),
+        compiler_params=params,
+        name="own",
+    )(core.reshape(1), own, vbig)
     return pl.pallas_call(
-        final_kernel,
-        in_specs=[pl.BlockSpec(memory_space=pltpu.SMEM), vmem, vmem] + [hbm] * len(held),
+        other_kernel,
+        in_specs=[smem, vmem, vmem, vmem, hbm],
         out_specs=hbm,
-        out_shape=jax.ShapeDtypeStruct((owned, 32, 256), jnp.bfloat16),
-        scratch_shapes=[
-            pltpu.VMEM((HALF, 32, 256), jnp.bfloat16),
-            pltpu.VMEM((4, HALF, 256), jnp.float32),
-            pltpu.VMEM(msg.shape, jnp.float32),
-            pltpu.SemaphoreType.DMA((HALF // BLOCK,)),
-        ],
-        input_output_aliases={3: 0} if held else {},
-        compiler_params=pltpu.CompilerParams(vmem_limit_bytes=LIMIT),
-        name="final",
-    )(share, msg, vbig, *held)
+        out_shape=whole,
+        scratch_shapes=scratch(HALF),
+        input_output_aliases={4: 0},
+        compiler_params=params,
+        name="other",
+    )((1 - core).reshape(1), other, vbig, rest, out)
 
 
 def exchange(blocks, n_pair, n_orb):
@@ -259,8 +301,7 @@
     blocks, vbig = select_stage(places, keep, recv, vir_coef[tile_index])
     own = exchange(blocks, n_pair, n_orb)
     other = lax.ppermute(own, "orb", other_core)
-    mine = final_stage(core.reshape(1), own, vbig, owned)
-    return final_stage((1 - core).reshape(1), other, vbig, owned, mine)
+    return final_stage(core, own, other, vbig, owned)
 
 
 def solution(mesh):

time: 48.4 us -> 47.9 us (0.990)
  transfers between devices with their start and end apart: 2 -> 2, of which waited for: 1 -> 1; matrix products, arithmetic and copies ran while one was open for 2% -> 2% of each run, Pallas kernels for 4% -> 3%
where the time goes in v5:
time: 47.9 us; the launch traced here: 47.8 us
  blocking collectives  28.3 us (59%)
  Pallas kernels  12.6 us (26%)
  starting transfers between devices  5.61 us (12%)
  local copies, waits for them, and re-layouts  0.9 us (2%)
    all_to_all x1, blocking collectives, exchange(): lax.all_to_all(packed, ('pair', 'orb'), 0, 0, axis_index_groups=groups, t...  28.3 us
    pallas_call x1, Pallas kernels, half_stage(): pl.pallas_call(half_kernel, grid=(np_ // block,), in_specs=[pl.BlockSpec(...  5.14 us
    pallas_call x1, Pallas kernels, select_stage(): pl.pallas_call(select_kernel, out_shape=[jax.ShapeDtypeStruct((lines, 128...  3.86 us
    ppermute x1, starting transfers between devices, on_device(): recv = lax.ppermute(send, 'orb', other_core)  3.22 us
    ppermute x1, starting transfers between devices, on_device(): other = lax.ppermute(own, 'orb', other_core)  2.38 us
    pallas_call x1, Pallas kernels, final_stage(): pl.pallas_call(other_kernel, in_specs=[smem, vmem, vmem, vmem, hbm], out_...  2.02 us
    pallas_call x1, Pallas kernels, final_stage(): pl.pallas_call(own_kernel, in_specs=[smem, vmem, vmem], out_specs=[hbm, v...  1.57 us
  transfers between devices with their start and end apart: 2, of which 1 were waited for; matrix products, arithmetic and copies ran while one was open for 2% of the time, Pallas kernels for 3%

profile of v5, /device:TPU:1, one launch (start us, length us, event | category | flops | bytes accessed | tf_op | source)
XLA Modules:
  0.0 47.8 jit_solution(1942230699369073167)
XLA Ops:
  0.0 0.0 copy-start
  0.0 0.0 copy-start.1
  0.0 0.0 copy-start.2
  0.0 5.1 %half.1 = (f32[640,256]{1,0:T(8,128)S(1)}, bf16[640,256]{1,0:T(8,128)(2,1)S(1)}) custom-call(s32[1]{0:T(128)} %bitcast.1.orb_ref, bf16[306,8,1224]{2,1,0:T(8,128)(2,1)} %bitcast.10, bf16[200,1224]{1,0:T(8,128)(2,1)} %bitcast.11), custom_call_target="tpu_custom_call" | custom-call | tf_op jit(solution)/shard_map/half/pallas_call | solution.py:76
  5.2 3.2 %collective-permute-start = (bf16[640,256]{1,0:T(8,128)(2,1)S(1)}, bf16[640,256]{1,0:T(8,128)(2,1)S(1)}, u32[]{:S(2)}, u32[]{:S(2)}) collective-permute-start(bf16[640,256]{1,0:T(8,128)(2,1)S(1)} %get-tuple-element.12), channel_id=1, source_target_pairs={{0,1},{1,0},{2,3},{3,2},{4,5},{5,4},{6,7},{7,6},{8,9},{9,8},{10,11... | collective-permute-start | bytes 983048 | tf_op jit(solution)/shard_map/ppermute | solution.py:299
  8.4 0.0 copy-done.1
  8.4 0.2 reshape.28
  8.6 0.1 fusion
  8.7 0.1 reshape.30
  8.8 0.0 copy-done.2
  8.9 0.0 copy-done
  8.9 0.6 %gather_fusion = bf16[16,256]{1,0:T(8,128)(2,1)S(1)} fusion(bf16[1224,256]{1,0:T(8,128)(2,1)S(1)} %copy-done, s32[1024]{0:T(1024)S(1)} %pad_clamp_fusion), kind=kCustom, calls=%fused_computation | custom fusion | bytes 16448 | tf_op jit(solution)/shard_map/gather | solution.py:301
  9.5 0.2 collective-permute-done.recv_ref
  9.6 3.9 %select.2 = (bf16[1280,128]{1,0:T(8,128)(2,1)S(1)}, bf16[256,256]{1,0:T(8,128)(2,1)S(1)}) custom-call(s32[4,2560]{1,0:T(4,128)S(1)} %reshape.31.place_ref, f32[640,256]{1,0:T(8,128)S(1)} %get-tuple-element.11.keep_ref, bf16[640,256]{1,0:T(8,128)(2,1)S(1)} %collective-permute-done.recv_ref, bf16[16,256]{1,0:T(8,128)(2,1)S(1)} %gather_fusion), custom_call_target="tpu_custom_call" | custom-call | tf_op jit(solution)/shard_map/select/pallas_call | solution.py:147
  13.5 28.3 %all_to_all.5 = bf16[128,5,2,128]{3,2,1,0:T(2,128)(2,1)S(1)} all-to-all(bf16[128,5,2,128]{3,2,1,0:T(2,128)(2,1)S(1)} %bitcast.9), channel_id=1, replica_groups={{0,2,4,6,8,10,12,14,16,18,20,22,24,26,28,30,32,34,36,38,40,42,44,46,48,..., dimensions={0} | all-to-all | bytes 655360 | tf_op jit(solution)/shard_map/all_to_all | solution.py:285
  41.8 2.4 %collective-permute-start.1 = (bf16[1280,128]{1,0:T(8,128)(2,1)S(1)}, bf16[1280,128]{1,0:T(8,128)(2,1)S(1)}, u32[]{:S(2)}, u32[]{:S(2)}) collective-permute-start(bf16[1280,128]{1,0:T(8,128)(2,1)S(1)} %bitcast.7), channel_id=1, source_target_pairs={{0,1},{1,0},{2,3},{3,2},{4,5},{5,4},{6,7},{7,6},{8,9},{9,8},{10,11... | collective-permute-start | bytes 983048 | tf_op jit(solution)/shard_map/ppermute | solution.py:303
  44.2 1.6 %own.1 = (bf16[315,32,256]{2,1,0:T(8,128)(2,1)}, bf16[80,32,256]{2,1,0:T(8,128)(2,1)S(1)}) custom-call(s32[1]{0:T(128)} %bitcast.6.share_ref, bf16[1280,128]{1,0:T(8,128)(2,1)S(1)} %bitcast.8, bf16[256,256]{1,0:T(8,128)(2,1)S(1)} %get-tuple-element.14.vbig_ref), custom_call_target="tpu_custom_call" | custom-call | tf_op jit(solution)/shard_map/own/pallas_call | solution.py:261
  45.8 0.0 collective-permute-done.1.msg_ref
  45.8 2.0 %other.1 = bf16[315,32,256]{2,1,0:T(8,128)(2,1)} custom-call(s32[1]{0:T(128)} %bitcast.share_ref, bf16[1280,128]{1,0:T(8,128)(2,1)S(1)} %collective-permute-done.1.msg_ref, bf16[256,256]{1,0:T(8,128)(2,1)S(1)} %get-tuple-element.14.vbig_ref, bf16[80,32,256]{2,1,0:T(8,128)(2,1)S(1)} %get-tuple-element.15.rest_ref, ...), custom_call_target="tpu_custom_call", output_to_operand_aliasing={{}: (4, {})} | custom-call | tf_op jit(solution)/shard_map/other/pallas_call | solution.py:270
  (7 shorter events, 0.0 us)
Async XLA Ops:
  0.0 8.9 %copy-start = (bf16[1224,256]{1,0:T(8,128)(2,1)S(1)}, bf16[1224,256]{1,0:T(8,128)(2,1)}, u32[]{:S(2)}) copy-start(bf16[1224,256]{1,0:T(8,128)(2,1)} %param.7) | copy-start | bytes 1880068
  0.0 8.4 %copy-start.1 = (s32[20160]{0:T(1024)S(1)}, s32[20160]{0:T(1024)}, u32[]{:S(2)}) copy-start(s32[20160]{0:T(1024)} %param.9) | copy-start | bytes 241924
  0.0 8.8 %copy-start.2 = (s32[16]{0:T(128)S(1)}, s32[16]{0:T(128)}, u32[]{:S(2)}) copy-start(s32[16]{0:T(128)} %param.8) | copy-start | bytes 196
  5.2 4.5 %collective-permute-start = (bf16[640,256]{1,0:T(8,128)(2,1)S(1)}, bf16[640,256]{1,0:T(8,128)(2,1)S(1)}, u32[]{:S(2)}, u32[]{:S(2)}) collective-permute-start(bf16[640,256]{1,0:T(8,128)(2,1)S(1)} %get-tuple-element.12), channel_id=1, source_target_pairs={{0,1},{1,0},{2,3},{3,2},{4,5},{5,4},{6,7},{7,6},{8,9},{9,8},{10,11... | collective-permute-start | bytes 983048 | tf_op jit(solution)/shard_map/ppermute | solution.py:299
  41.8 4.0 %collective-permute-start.1 = (bf16[1280,128]{1,0:T(8,128)(2,1)S(1)}, bf16[1280,128]{1,0:T(8,128)(2,1)S(1)}, u32[]{:S(2)}, u32[]{:S(2)}) collective-permute-start(bf16[1280,128]{1,0:T(8,128)(2,1)S(1)} %bitcast.7), channel_id=1, source_target_pairs={{0,1},{1,0},{2,3},{3,2},{4,5},{5,4},{6,7},{7,6},{8,9},{9,8},{10,11... | collective-permute-start | bytes 983048 | tf_op jit(solution)/shard_map/ppermute | solution.py:303

commit v6 on v5

--- a/solution.py
+++ b/solution.py
@@ -112,17 +112,19 @@
     col_ref[...] = col
     lane = lax.broadcasted_iota(jnp.int32, (KK, 128), 1)
     kpos = lax.broadcasted_iota(jnp.int32, (KK, 128), 0)
-    first_col = lax.broadcasted_iota(jnp.int32, (8, CHUNK), 0)
+    first_col = lax.broadcasted_iota(jnp.int16, (16, CHUNK), 0)
     for ch in range(place_ref.shape[0]):
         row = row_ref[ch:ch + 1, :]
         col = col_ref[ch:ch + 1, :]
         same = lax.broadcasted_iota(jnp.int16, (ROWS, CHUNK), 0) == row.astype(jnp.int16)
         hot = jnp.where(same, jnp.ones((), jnp.bfloat16), jnp.zeros((), jnp.bfloat16))
-        picked = jnp.dot(tri_ref[...], hot, preferred_element_type=jnp.float32)
-        accs = [jnp.zeros((8, CHUNK), jnp.float32)] * KK
-        for v in range(COLS // 8):
-            here = first_col + 8 * v == col
-            accs = [jnp.where(here, picked[k * COLS + 8 * v:k * COLS + 8 * v + 8], a) for k, a in enumerate(accs)]
+        picked = jnp.dot(tri_ref[...], hot, preferred_element_type=jnp.float32).astype(jnp.bfloat16)
+        narrow = col.astype(jnp.int16)
+        accs = [jnp.zeros((16, CHUNK), jnp.bfloat16)] * KK
+        for v in range(COLS // 16):
+            here = first_col + jnp.int16(16 * v) == narrow
+            accs = [jnp.where(here, picked[k * COLS + 16 * v:k * COLS + 16 * v + 16], a) for k, a in enumerate(accs)]
+        accs = [a.astype(jnp.float32) for a in accs]
         vals = jnp.concatenate([jnp.sum(a, axis=0, keepdims=True) for a in accs], axis=0)
         for u in range(CHUNK // 640):
             left = vals[:, 640 * u + 512:640 * u + 640]

time: 47.9 us -> 47.8 us (level)
  no operation moved by 1% of the time
where the time goes in v6:
time: 47.8 us; the launch traced here: 47.7 us
  blocking collectives  28.3 us (59%)
  Pallas kernels  12.5 us (26%)
  starting transfers between devices  5.6 us (12%)
  local copies, waits for them, and re-layouts  0.9 us (2%)
    all_to_all x1, blocking collectives, exchange(): lax.all_to_all(packed, ('pair', 'orb'), 0, 0, axis_index_groups=groups, t...  28.3 us
    pallas_call x1, Pallas kernels, half_stage(): pl.pallas_call(half_kernel, grid=(np_ // block,), in_specs=[pl.BlockSpec(...  5.14 us
    pallas_call x1, Pallas kernels, select_stage(): pl.pallas_call(select_kernel, out_shape=[jax.ShapeDtypeStruct((lines, 128...  3.73 us
    ppermute x1, starting transfers between devices, on_device(): recv = lax.ppermute(send, 'orb', other_core)  3.22 us
    ppermute x1, starting transfers between devices, on_device(): other = lax.ppermute(own, 'orb', other_core)  2.37 us
    pallas_call x1, Pallas kernels, final_stage(): pl.pallas_call(other_kernel, in_specs=[smem, vmem, vmem, vmem, hbm], out_...  2.01 us
    pallas_call x1, Pallas kernels, final_stage(): pl.pallas_call(own_kernel, in_specs=[smem, vmem, vmem], out_specs=[hbm, v...  1.57 us
  transfers between devices with their start and end apart: 2, of which 1 were waited for; matrix products, arithmetic and copies ran while one was open for 2% of the time, Pallas kernels for 3%

profile of v6, /device:TPU:1, one launch (start us, length us, event | category | flops | bytes accessed | tf_op | source)
XLA Modules:
  0.0 47.7 jit_solution(5801296481917922910)
XLA Ops:
  0.0 0.0 copy-start
  0.0 0.0 copy-start.1
  0.0 0.0 copy-start.2
  0.0 5.1 %half.1 = (f32[640,256]{1,0:T(8,128)S(1)}, bf16[640,256]{1,0:T(8,128)(2,1)S(1)}) custom-call(s32[1]{0:T(128)} %bitcast.1.orb_ref, bf16[306,8,1224]{2,1,0:T(8,128)(2,1)} %bitcast.10, bf16[200,1224]{1,0:T(8,128)(2,1)} %bitcast.11), custom_call_target="tpu_custom_call" | custom-call | tf_op jit(solution)/shard_map/half/pallas_call | solution.py:76
  5.2 3.2 %collective-permute-start = (bf16[640,256]{1,0:T(8,128)(2,1)S(1)}, bf16[640,256]{1,0:T(8,128)(2,1)S(1)}, u32[]{:S(2)}, u32[]{:S(2)}) collective-permute-start(bf16[640,256]{1,0:T(8,128)(2,1)S(1)} %get-tuple-element.12), channel_id=1, source_target_pairs={{0,1},{1,0},{2,3},{3,2},{4,5},{5,4},{6,7},{7,6},{8,9},{9,8},{10,11... | collective-permute-start | bytes 983048 | tf_op jit(solution)/shard_map/ppermute | solution.py:301
  8.4 0.0 copy-done.1
  8.4 0.2 reshape.28
  8.6 0.1 fusion
  8.7 0.1 reshape.30
  8.8 0.0 copy-done.2
  8.9 0.0 copy-done
  8.9 0.6 %gather_fusion = bf16[16,256]{1,0:T(8,128)(2,1)S(1)} fusion(bf16[1224,256]{1,0:T(8,128)(2,1)S(1)} %copy-done, s32[1024]{0:T(1024)S(1)} %pad_clamp_fusion), kind=kCustom, calls=%fused_computation | custom fusion | bytes 16448 | tf_op jit(solution)/shard_map/gather | solution.py:303
  9.5 0.2 collective-permute-done.recv_ref
  9.6 3.7 %select.2 = (bf16[1280,128]{1,0:T(8,128)(2,1)S(1)}, bf16[256,256]{1,0:T(8,128)(2,1)S(1)}) custom-call(s32[4,2560]{1,0:T(4,128)S(1)} %reshape.31.place_ref, f32[640,256]{1,0:T(8,128)S(1)} %get-tuple-element.11.keep_ref, bf16[640,256]{1,0:T(8,128)(2,1)S(1)} %collective-permute-done.recv_ref, bf16[16,256]{1,0:T(8,128)(2,1)S(1)} %gather_fusion), custom_call_target="tpu_custom_call" | custom-call | tf_op jit(solution)/shard_map/select/pallas_call | solution.py:149
  13.4 28.3 %all_to_all.5 = bf16[128,5,2,128]{3,2,1,0:T(2,128)(2,1)S(1)} all-to-all(bf16[128,5,2,128]{3,2,1,0:T(2,128)(2,1)S(1)} %bitcast.9), channel_id=1, replica_groups={{0,2,4,6,8,10,12,14,16,18,20,22,24,26,28,30,32,34,36,38,40,42,44,46,48,..., dimensions={0} | all-to-all | bytes 655360 | tf_op jit(solution)/shard_map/all_to_all | solution.py:287
  41.7 2.4 %collective-permute-start.1 = (bf16[1280,128]{1,0:T(8,128)(2,1)S(1)}, bf16[1280,128]{1,0:T(8,128)(2,1)S(1)}, u32[]{:S(2)}, u32[]{:S(2)}) collective-permute-start(bf16[1280,128]{1,0:T(8,128)(2,1)S(1)} %bitcast.7), channel_id=1, source_target_pairs={{0,1},{1,0},{2,3},{3,2},{4,5},{5,4},{6,7},{7,6},{8,9},{9,8},{10,11... | collective-permute-start | bytes 983048 | tf_op jit(solution)/shard_map/ppermute | solution.py:305
  44.1 1.6 %own.1 = (bf16[315,32,256]{2,1,0:T(8,128)(2,1)}, bf16[80,32,256]{2,1,0:T(8,128)(2,1)S(1)}) custom-call(s32[1]{0:T(128)} %bitcast.6.share_ref, bf16[1280,128]{1,0:T(8,128)(2,1)S(1)} %bitcast.8, bf16[256,256]{1,0:T(8,128)(2,1)S(1)} %get-tuple-element.14.vbig_ref), custom_call_target="tpu_custom_call" | custom-call | tf_op jit(solution)/shard_map/own/pallas_call | solution.py:263
  45.7 0.0 collective-permute-done.1.msg_ref
  45.7 2.0 %other.1 = bf16[315,32,256]{2,1,0:T(8,128)(2,1)} custom-call(s32[1]{0:T(128)} %bitcast.share_ref, bf16[1280,128]{1,0:T(8,128)(2,1)S(1)} %collective-permute-done.1.msg_ref, bf16[256,256]{1,0:T(8,128)(2,1)S(1)} %get-tuple-element.14.vbig_ref, bf16[80,32,256]{2,1,0:T(8,128)(2,1)S(1)} %get-tuple-element.15.rest_ref, ...), custom_call_target="tpu_custom_call", output_to_operand_aliasing={{}: (4, {})} | custom-call | tf_op jit(solution)/shard_map/other/pallas_call | solution.py:272
  (7 shorter events, 0.0 us)
Async XLA Ops:
  0.0 8.9 %copy-start = (bf16[1224,256]{1,0:T(8,128)(2,1)S(1)}, bf16[1224,256]{1,0:T(8,128)(2,1)}, u32[]{:S(2)}) copy-start(bf16[1224,256]{1,0:T(8,128)(2,1)} %param.7) | copy-start | bytes 1880068
  0.0 8.4 %copy-start.1 = (s32[20160]{0:T(1024)S(1)}, s32[20160]{0:T(1024)}, u32[]{:S(2)}) copy-start(s32[20160]{0:T(1024)} %param.9) | copy-start | bytes 241924
  0.0 8.8 %copy-start.2 = (s32[16]{0:T(128)S(1)}, s32[16]{0:T(128)}, u32[]{:S(2)}) copy-start(s32[16]{0:T(128)} %param.8) | copy-start | bytes 196
  5.2 4.5 %collective-permute-start = (bf16[640,256]{1,0:T(8,128)(2,1)S(1)}, bf16[640,256]{1,0:T(8,128)(2,1)S(1)}, u32[]{:S(2)}, u32[]{:S(2)}) collective-permute-start(bf16[640,256]{1,0:T(8,128)(2,1)S(1)} %get-tuple-element.12), channel_id=1, source_target_pairs={{0,1},{1,0},{2,3},{3,2},{4,5},{5,4},{6,7},{7,6},{8,9},{9,8},{10,11... | collective-permute-start | bytes 983048 | tf_op jit(solution)/shard_map/ppermute | solution.py:301
  41.7 4.0 %collective-permute-start.1 = (bf16[1280,128]{1,0:T(8,128)(2,1)S(1)}, bf16[1280,128]{1,0:T(8,128)(2,1)S(1)}, u32[]{:S(2)}, u32[]{:S(2)}) collective-permute-start(bf16[1280,128]{1,0:T(8,128)(2,1)S(1)} %bitcast.7), channel_id=1, source_target_pairs={{0,1},{1,0},{2,3},{3,2},{4,5},{5,4},{6,7},{7,6},{8,9},{9,8},{10,11... | collective-permute-start | bytes 983048 | tf_op jit(solution)/shard_map/ppermute | solution.py:305
